TPU v7x, 32 devices: a whole 2x2x4 slice. The times are simulated.
32 devices in a mesh: dp: 16 (over z, y, core), tensor: 2 (over x).
Axes of the slice: x: 2, y: 2, z: 4, core: 2. Of those that a mesh axis runs over, the one named last changes fastest.
Arguments:
- queries: bfloat16 [8192, 2048], P('dp', 'tensor'), may hold values from -360 to 360
- neighbours: int32 [128, 2], P('dp'), may hold values from 0 to 15, as said below
- counts: int32 [128], P('dp'), may hold values from 1 to 2
- states: bfloat16 [16, 128, 4096], P('dp'), may hold values from -6 to 6
- w_key: bfloat16 [4096, 2048], P('dp', 'tensor'), may hold values from -0.09375 to 0.09375
- w_value: bfloat16 [4096, 2048], P('dp', 'tensor'), may hold values from -0.09375 to 0.09375
- cotangent: bfloat16 [8192, 2048], P('dp', 'tensor'), may hold values from -6 to 6
Outputs:
- context: bfloat16 [8192, 2048], P('dp', 'tensor')
- query_grad: bfloat16 [8192, 2048], P('dp', 'tensor')
- state_grad: bfloat16 [16, 128, 4096], P('dp', None, 'tensor')
Inputs may be any that keep to these rules, and one draw needn't show every extreme that they name: Neighbour n is held by dp index n. Among the 16 slots of one index of dp, at most 1 name neighbours of one holder, and some holder is named exactly 1 times.
All inputs are finite; a program needn't handle non-finite values.
Results may differ from a plain program's by a relative error of at most 0.035.
The roundings to bfloat16 on the way count: a program that leaves them out, or rounds other values in their place, can miss the bound.
Values may be sent and summed in bfloat16 or wider, within the bound.
No kernel may reach another device: no remote copies, remote signals or barrier semaphores. Data moves between devices by JAX's collectives and lax.ppermute only.
A program may use at most 128 MiB of HBM per device.

v0:
```python
import math

import jax
import jax.numpy as jnp
from jax import lax
from jax.sharding import PartitionSpec as P

HEAD = 128


def local(queries, neighbours, counts, states, w_key, w_value, cotangent):
    dp_count = lax.axis_size("dp")
    spans, neigh = neighbours.shape
    slots = spans * neigh
    capacity = (slots + dp_count - 1) // dp_count
    buffer_rows = dp_count * capacity
    nbr_dev, nbr_len, dmodel = states.shape
    local_width = queries.shape[1]
    heads_here = local_width // HEAD
    span_len = queries.shape[0] // spans
    score_scale = 1.0 / math.sqrt(HEAD)
    slot_ids = neighbours.reshape(slots)
    holder = slot_ids // nbr_dev
    slot_order = jnp.arange(slots, dtype=jnp.int32)
    earlier = (holder[:, None] == holder[None, :]) & (slot_order[None, :] < slot_order[:, None])
    holder_rank = jnp.sum(earlier.astype(jnp.int32), axis=1)
    position = holder * capacity + holder_rank
    placing = position[None, :] == jnp.arange(buffer_rows, dtype=jnp.int32)[:, None]
    place_half = placing.astype(jnp.bfloat16)
    place_full = placing.astype(jnp.float32)
    query_spans = queries.reshape(spans, 1, span_len * local_width)
    query_slots = jnp.broadcast_to(query_spans, (spans, neigh, span_len * local_width)).reshape(
        slots, span_len * local_width
    )
    send_query = jnp.dot(place_half, query_slots, preferred_element_type=jnp.float32).astype(
        jnp.bfloat16
    )
    send_query = send_query.reshape(dp_count, capacity, span_len, local_width)
    flat_states = states.reshape(nbr_dev * nbr_len, dmodel)
    key_full = lax.all_gather(w_key, "dp", axis=0, tiled=True)
    value_full = lax.all_gather(w_value, "dp", axis=0, tiled=True)
    key_acc = jnp.dot(flat_states, key_full, preferred_element_type=jnp.float32)
    value_acc = jnp.dot(flat_states, value_full, preferred_element_type=jnp.float32)
    key_rows = key_acc.astype(jnp.bfloat16).reshape(nbr_len, heads_here, HEAD)
    value_rows = value_acc.astype(jnp.bfloat16).reshape(nbr_len, heads_here, HEAD)
    key_rows, value_rows, key_full, value_full = (key_rows, value_rows, key_full, value_full)
    recv_query = lax.all_to_all(send_query, "dp", split_axis=0, concat_axis=0, tiled=True)
    lead = recv_query.shape[:-1]
    item_query = recv_query.reshape(lead + (heads_here, HEAD))
    scores = (
        jnp.einsum("abqhd,khd->abqhk", item_query, key_rows, preferred_element_type=jnp.float32)
        * score_scale
    )
    row_max = jnp.max(scores, axis=-1, keepdims=True)
    log_total = row_max[..., 0] + jnp.log(jnp.sum(jnp.exp(scores - row_max), axis=-1))
    prob_out = jnp.exp(scores - log_total[..., None])
    part_out = jnp.einsum(
        "abqhk,khd->abqhd",
        prob_out.astype(jnp.bfloat16),
        value_rows,
        preferred_element_type=jnp.float32,
    ).astype(jnp.bfloat16)
    item_part = part_out.reshape(lead + (local_width,))
    item_query = recv_query.reshape(dp_count, capacity, span_len, heads_here, HEAD)
    prob_half = prob_out.astype(jnp.bfloat16)
    back_part, back_log = (
        lax.all_to_all(
            item_part.astype(jnp.float32), "dp", split_axis=0, concat_axis=0, tiled=True
        ).astype(item_part.dtype),
        lax.all_to_all(log_total, "dp", split_axis=0, concat_axis=0, tiled=True),
    )
    back_part = back_part.reshape(buffer_rows, span_len, local_width)
    back_log = back_log.reshape(buffer_rows, span_len, heads_here)
    got_part = back_part[position].reshape(spans, neigh, span_len, heads_here, HEAD)
    got_log = back_log[position].reshape(spans, neigh, span_len, heads_here)
    is_valid = jnp.arange(neigh, dtype=jnp.int32)[None, :] < counts[:, None]
    live = is_valid[:, :, None, None]
    masked = jnp.where(live, got_log, -1e30)
    top_part = jnp.max(masked, axis=1, keepdims=True)
    raw_weight = jnp.where(live, jnp.exp(masked - top_part), 0.0)
    mix_weight = raw_weight / jnp.sum(raw_weight, axis=1, keepdims=True)
    part_full = got_part.astype(jnp.float32)
    mixed_rows = jnp.sum(mix_weight[..., None] * part_full, axis=1)
    context = mixed_rows.astype(jnp.bfloat16).reshape(spans * span_len, local_width)
    grad_rows = cotangent.astype(jnp.float32).reshape(spans, span_len, heads_here, HEAD)
    part_grad = lax.optimization_barrier(
        (mix_weight[..., None] * grad_rows[:, None]).astype(jnp.bfloat16)
    )
    lse_grad = mix_weight * jnp.sum(grad_rows[:, None] * (part_full - mixed_rows[:, None]), axis=-1)
    rest_term = jnp.sum(part_grad.astype(jnp.float32) * part_full, axis=-1) - lse_grad
    send_grad = jnp.dot(
        place_half,
        part_grad.reshape(slots, span_len * local_width),
        preferred_element_type=jnp.float32,
    ).astype(jnp.bfloat16)
    send_grad = send_grad.reshape(dp_count, capacity, span_len, local_width)
    send_rest = jnp.dot(
        place_full, rest_term.reshape(slots, span_len * heads_here), precision=lax.Precision.HIGHEST
    )
    send_rest = send_rest.reshape(dp_count, capacity, span_len, heads_here)
    recv_grad, recv_rest = (
        lax.all_to_all(
            send_grad.astype(jnp.float32), "dp", split_axis=0, concat_axis=0, tiled=True
        ).astype(send_grad.dtype),
        lax.all_to_all(send_rest, "dp", split_axis=0, concat_axis=0, tiled=True),
    )
    item_grad = recv_grad.reshape(dp_count, capacity, span_len, heads_here, HEAD)
    dprob = jnp.einsum(
        "abqhd,khd->abqhk", item_grad, value_rows, preferred_element_type=jnp.float32
    )
    dscore = prob_out * (dprob - recv_rest[..., None])
    dscore_half = dscore.astype(jnp.bfloat16)
    item_dq = (
        jnp.einsum("abqhk,khd->abqhd", dscore_half, key_rows, preferred_element_type=jnp.float32)
        * score_scale
    )
    item_dq = item_dq.astype(jnp.bfloat16).reshape(dp_count, capacity, span_len, local_width)
    back_dq = lax.all_to_all(item_dq, "dp", split_axis=0, concat_axis=0, tiled=True)
    key_grad = (
        jnp.einsum("abqhk,abqhd->khd", dscore_half, item_query, preferred_element_type=jnp.float32)
        * score_scale
    )
    key_grad = key_grad.astype(jnp.bfloat16).reshape(nbr_dev * nbr_len, local_width)
    value_grad = jnp.einsum(
        "abqhk,abqhd->khd", prob_half, item_grad, preferred_element_type=jnp.float32
    )
    value_grad = value_grad.astype(jnp.bfloat16).reshape(nbr_dev * nbr_len, local_width)
    contract = (((1,), (1,)), ((), ()))
    state_term = lax.dot_general(key_grad, key_full, contract, preferred_element_type=jnp.float32)
    state_term = state_term + lax.dot_general(
        value_grad, value_full, contract, preferred_element_type=jnp.float32
    )
    summed = lax.psum_scatter(
        state_term.astype(jnp.bfloat16), "tensor", scatter_dimension=1, tiled=True
    ).astype(jnp.float32)
    state_grad = summed.astype(jnp.bfloat16).reshape(nbr_dev, nbr_len, summed.shape[1])
    got_dq = back_dq.reshape(buffer_rows, span_len * local_width)[position]
    got_dq = got_dq.reshape(spans, neigh, span_len * local_width).astype(jnp.float32)
    query_grad = jnp.sum(got_dq, axis=1).astype(jnp.bfloat16).reshape(spans * span_len, local_width)
    return (context, query_grad, state_grad)


def solution(mesh):
    placed = (
        P("dp", "tensor"),
        P("dp", None),
        P("dp"),
        P("dp", None, None),
        P("dp", "tensor"),
        P("dp", "tensor"),
        P("dp", "tensor"),
    )
    return jax.shard_map(
        local,
        mesh=mesh,
        in_specs=placed,
        out_specs=(P("dp", "tensor"), P("dp", "tensor"), P("dp", None, "tensor")),
        check_vma=False,
    )
```

profile of v0, /device:TPU:13, one launch (start us, length us, event | category | flops | bytes accessed | tf_op | source)
XLA Modules:
  0.0 464.8 jit_solution(14205762382722877230)
XLA Ops:
  9.7 2.7 broadcast_in_dim.29
  12.4 2.3 broadcast_in_dim.30
  14.7 1.9 reshape.262
  16.5 2.3 convolution_convert_fusion.1
  20.0 95.7 %all_to_all.30 = bf16[16,1,64,1024]{3,2,1,0:T(8,128)(2,1)S(1)} all-to-all(bf16[16,1,64,1024]{3,2,1,0:T(8,128)(2,1)S(1)} %bitcast.235), channel_id=1, replica_groups=mesh['dp'=16,'tensor'=2] {'dp'}, dimensions={0} | all-to-all | bytes 4194304 | tf_op jit(solution)/shard_map/all_to_all | solution.py:47
  116.3 1.4 copy-done.7
  118.3 4.6 fusion.26
  125.6 2.3 fusion.3
  128.7 7.7 %all-to-all-start.1 = ((f32[16,1,512]{2,1,0:T(1,128)}), f32[16,1,512]{2,1,0:T(1,128)S(1)}, u32[]{:S(2)}, u32[]{:S(2)}) async-start(f32[16,1,512]{2,1,0:T(1,128)} %reshape.325), calls=%async_computation.1 | async-start | bytes 65536 | tf_op jit(solution)/shard_map/all_to_all | solution.py:70
  136.4 2.9 fusion.5
  139.3 57.3 %all-gather.5.cloned.1.call-done = bf16[4096,1024]{1,0:T(8,128)(2,1)} async-done(((bf16[256,1024]{1,0:T(8,128)(2,1)}), bf16[4096,1024]{1,0:T(8,128)(2,1)}) %all-gather.5.cloned.1.call-update) | async-done | bytes 8388624 | tf_op jit(solution)/shard_map/all_gather | solution.py:41
  196.6 4.6 fusion.27
  202.5 3.3 copy.86
  205.8 5.5 %convert_bitcast_fusion.2 = bf16[16,64,1,1024]{3,2,1,0:T(2,128)(2,1)} fusion(f32[16,1,64,1024]{3,1,2,0:T(1,128)S(1)} %bitcast.218), kind=kLoop, calls=%fused_computation.77 | loop fusion | flops 1048576 | bytes 6291456
  211.8 14.0 %reduce.4 = bf16[16,64,1024]{2,1,0:T(8,128)(2,1)S(1)} reduce(bf16[16,64,1,1024]{3,2,1,0:T(2,128)(2,1)} %convert_bitcast_fusion.2, bf16[]{:T(256)} %broadcast.138), dimensions={2}, to_apply=%convert_bitcast_fusion.2.reduce_sub_computation | reduce | bytes 4194306
  225.8 2.8 reshape.323
  228.6 5.9 %all-to-all-start.2 = ((bf16[16,2,32768]{2,1,0:T(2,128)(2,1)}), bf16[16,2,32768]{2,1,0:T(2,128)(2,1)S(1)}, u32[]{:S(2)}, u32[]{:S(2)}) async-start(bf16[16,2,32768]{2,1,0:T(2,128)(2,1)} %reshape.323), calls=%async_computation.2 | async-start | bytes 4194304 | tf_op jit(solution)/shard_map/all_to_all | solution.py:67
  235.0 1.8 copy.111
  240.2 1.3 sub.63
  242.5 1.9 div.23
  245.4 36.4 %all-to-all-done.2 = bf16[16,2,32768]{2,1,0:T(2,128)(2,1)S(1)} async-done(((bf16[16,2,32768]{2,1,0:T(2,128)(2,1)}), bf16[16,2,32768]{2,1,0:T(2,128)(2,1)S(1)}, u32[]{:S(2)}, u32[]{:S(2)}) %all-to-all-start.2) | async-done | bytes 2097184 | tf_op jit(solution)/shard_map/all_to_all | solution.py:67
  281.8 6.8 %reshape.324 = bf16[16,64,1,1024]{3,2,1,0:T(2,128)(2,1)} reshape(bf16[16,2,32768]{2,1,0:T(2,128)(2,1)S(1)} %all-to-all-done.2) | data formatting | bytes 4194304
  288.6 3.0 copy.142
  291.6 2.0 gather_fusion.1
  293.6 2.3 copy.109
  296.0 4.0 multiply_convert_fusion.2
  300.0 3.1 reshape.271
  303.1 5.8 %multiply_reduce_fusion = (f32[8,2,64,8]{3,2,1,0:T(8,128)S(1)}, f32[8,2,64,8]{3,2,1,0:T(8,128)S(1)}) fusion(f32[8,2,64,8,128]{4,3,2,1,0:T(8,128)} %bitcast.214, f32[8,64,8,128]{3,2,1,0:T(8,128)S(1)} %get-tuple-element.6, f32[8,64,8,128]{3,2,1,0:T(8,128)} %bitcast.215, bf16[8,2,64,8,128]{4,3,2,1,0:T(8,128)(2,1)} %get-tuple-element.5), kind=kLoop, calls=%fused_computation.17 | loop fusion | flops 6275072 | bytes 10551296 | tf_op jit(solution)/shard_map/reduce_sum | solution.py:89
  312.2 4.9 %all-to-all-start.4 = ((f32[16,1,512]{2,1,0:T(1,128)}), f32[16,1,512]{2,1,0:T(1,128)S(1)}, u32[]{:S(2)}, u32[]{:S(2)}) async-start(f32[16,1,512]{2,1,0:T(1,128)} %reshape.327), calls=%async_computation.4 | async-start | bytes 65536 | tf_op jit(solution)/shard_map/all_to_all | solution.py:105
  317.1 2.3 fusion
  319.3 2.5 copy.112
  321.8 6.5 %all-to-all-start.3 = ((bf16[16,1,64,1024]{3,2,1,0:T(8,128)(2,1)}), bf16[16,1,64,1024]{3,2,1,0:T(8,128)(2,1)}, u32[]{:S(2)}, u32[]{:S(2)}) async-start(bf16[16,1,64,1024]{3,2,1,0:T(8,128)(2,1)} %bitcast.231), calls=%async_computation.3 | async-start | bytes 4194304 | tf_op jit(solution)/shard_map/all_to_all | solution.py:102
  329.1 46.6 %all-to-all-done.3 = bf16[16,1,64,1024]{3,2,1,0:T(8,128)(2,1)} async-done(((bf16[16,1,64,1024]{3,2,1,0:T(8,128)(2,1)}), bf16[16,1,64,1024]{3,2,1,0:T(8,128)(2,1)}, u32[]{:S(2)}, u32[]{:S(2)}) %all-to-all-start.3) | async-done | bytes 2097184 | tf_op jit(solution)/shard_map/all_to_all | solution.py:102
  375.7 2.2 copy.113
  380.0 1.5 copy-done.3
  381.5 2.5 multiply_convert_fusion.1
  385.3 1.8 bitcast_bitcast_fusion
  387.2 4.9 %all-to-all-start.5 = ((bf16[16,1,64,1024]{3,2,1,0:T(8,128)(2,1)}), bf16[16,1,64,1024]{3,2,1,0:T(8,128)(2,1)}, u32[]{:S(2)}, u32[]{:S(2)}) async-start(bf16[16,1,64,1024]{3,2,1,0:T(8,128)(2,1)} %bitcast_bitcast_fusion), calls=%async_computation.5 | async-start | bytes 4194304 | tf_op jit(solution)/shard_map/all_to_all | solution.py:118
  392.1 3.2 fusion.20
  396.5 6.7 %fusion.54 = f32[128,4096]{1,0:T(8,128)S(1)} fusion(bf16[128,1024]{0,1:T(8,128)(2,1)S(1)} %bitcast.246, bf16[4096,1024]{1,0:T(8,128)(2,1)} %all-gather.3.cloned.1.call-done), kind=kOutput, calls=%fused_computation.82 | convolution fusion | flops 1073741824 | bytes 10747904 | tf_op jit(solution)/shard_map/dot_general | solution.py:129
  403.2 3.9 fusion.1
  407.3 1.3 copy.143
  408.5 31.0 %all-to-all-done.5 = bf16[16,1,64,1024]{3,2,1,0:T(8,128)(2,1)} async-done(((bf16[16,1,64,1024]{3,2,1,0:T(8,128)(2,1)}), bf16[16,1,64,1024]{3,2,1,0:T(8,128)(2,1)}, u32[]{:S(2)}, u32[]{:S(2)}) %all-to-all-start.5) | async-done | bytes 2097184 | tf_op jit(solution)/shard_map/all_to_all | solution.py:118
  439.6 2.7 copy.114
  442.3 3.3 gather_fusion.2
  445.6 2.9 reshape.278
  448.5 6.7 %reduce_sum.81 = bf16[8,65536]{1,0:T(8,128)(2,1)} reduce(bf16[8,2,65536]{2,1,0:T(2,128)(2,1)S(1)} %reshape.278, bf16[]{:T(256)} %constant.30.clone.1), dimensions={1}, to_apply=%region_8.9 | reduce | flops 524288 | bytes 3145730 | tf_op jit(solution)/shard_map/reduce_sum | solution.py:139
  455.1 2.7 reshape.279
  (97 shorter events, 24.7 us)
Async XLA Ops:
  7.2 111.1 %copy-start = (bf16[1,128,4096]{2,1,0:T(8,128)(2,1)S(1)}, bf16[1,128,4096]{2,1,0:T(8,128)(2,1)}, u32[]{:S(2)}) copy-start(bf16[1,128,4096]{2,1,0:T(8,128)(2,1)} %param.10) | copy-start | bytes 3145732
  7.2 111.1 %all-gather.3.cloned.1.call-start = ((), (), s32[]{:S(2)}) async-start(), calls=%async_computation.7 | async-start | bytes 8912896 | tf_op jit(solution)/shard_map/all_gather | solution.py:40
  7.9 188.7 %all-gather.5.cloned.1.call-start = ((), (), s32[]{:S(2)}) async-start(), calls=%async_computation.8 | async-start | bytes 8912896 | tf_op jit(solution)/shard_map/all_gather | solution.py:41
  116.3 1.4 copy-start.7
  123.6 1.9 copy-start.2
  128.7 99.9 %all-to-all-start.1 = ((f32[16,1,512]{2,1,0:T(1,128)}), f32[16,1,512]{2,1,0:T(1,128)S(1)}, u32[]{:S(2)}, u32[]{:S(2)}) async-start(f32[16,1,512]{2,1,0:T(1,128)} %reshape.325), calls=%async_computation.1 | async-start | bytes 65536 | tf_op jit(solution)/shard_map/all_to_all | solution.py:70
  139.2 62.0 %copy-start.6 = (bf16[16,1,64,8,128]{4,2,0,3,1:T(8,128)(2,1)}, bf16[16,1,64,8,128]{4,2,0,3,1:T(8,128)(2,1)S(1)}, u32[]{:S(2)}) copy-start(bf16[16,1,64,8,128]{4,2,0,3,1:T(8,128)(2,1)S(1)} %fusion.5) | copy-start | bytes 6291460
  201.2 0.7 copy-start.12
  228.6 6.0 %copy-start.16 = (s32[8]{0:T(128)S(1)}, s32[8]{0:T(128)}, u32[]{:S(2)}) copy-start(s32[8]{0:T(128)} %param.9) | copy-start | bytes 100
  228.6 6.1 %copy-start.15 = (bf16[512,1024]{1,0:T(8,128)(2,1)S(1)}, bf16[512,1024]{1,0:T(8,128)(2,1)}, u32[]{:S(2)}) copy-start(bf16[512,1024]{1,0:T(8,128)(2,1)} %param.13) | copy-start | bytes 3145732
  228.6 53.2 %all-to-all-start.2 = ((bf16[16,2,32768]{2,1,0:T(2,128)(2,1)}), bf16[16,2,32768]{2,1,0:T(2,128)(2,1)S(1)}, u32[]{:S(2)}, u32[]{:S(2)}) async-start(bf16[16,2,32768]{2,1,0:T(2,128)(2,1)} %reshape.323), calls=%async_computation.2 | async-start | bytes 4194304 | tf_op jit(solution)/shard_map/all_to_all | solution.py:67
  293.6 2.4 copy-start.5
  293.6 2.4 copy-start.14
  295.9 4.0 copy-start.4
  312.2 9.7 %all-to-all-start.4 = ((f32[16,1,512]{2,1,0:T(1,128)}), f32[16,1,512]{2,1,0:T(1,128)S(1)}, u32[]{:S(2)}, u32[]{:S(2)}) async-start(f32[16,1,512]{2,1,0:T(1,128)} %reshape.327), calls=%async_computation.4 | async-start | bytes 65536 | tf_op jit(solution)/shard_map/all_to_all | solution.py:105
  321.8 53.9 %all-to-all-start.3 = ((bf16[16,1,64,1024]{3,2,1,0:T(8,128)(2,1)}), bf16[16,1,64,1024]{3,2,1,0:T(8,128)(2,1)}, u32[]{:S(2)}, u32[]{:S(2)}) async-start(bf16[16,1,64,1024]{3,2,1,0:T(8,128)(2,1)} %bitcast.231), calls=%async_computation.3 | async-start | bytes 4194304 | tf_op jit(solution)/shard_map/all_to_all | solution.py:102
  377.9 1.3 copy-start.9
  378.0 1.3 copy-start.13
  379.3 2.2 copy-start.3
  384.0 1.3 copy-start.10
  387.2 52.4 %all-to-all-start.5 = ((bf16[16,1,64,1024]{3,2,1,0:T(8,128)(2,1)}), bf16[16,1,64,1024]{3,2,1,0:T(8,128)(2,1)}, u32[]{:S(2)}, u32[]{:S(2)}) async-start(bf16[16,1,64,1024]{3,2,1,0:T(8,128)(2,1)} %bitcast_bitcast_fusion), calls=%async_computation.5 | async-start | bytes 4194304 | tf_op jit(solution)/shard_map/all_to_all | solution.py:118
  392.0 65.8 %reduce-scatter.2.cloned.1.call-start = ((), (), s32[]{:S(2)}) async-start(), calls=%async_computation.9 | async-start | bytes 1572864 | tf_op jit(solution)/shard_map/reduce_scatter | solution.py:133
  392.1 3.3 copy-start.8
  392.1 3.5 copy-start.11
  395.6 7.6 %slice-start = ((s8[8388608]{0:T(1024)(128)(4,1)}), s8[4194304]{0:T(1024)(128)(4,1)S(1)}, s32[]{:S(2)}) async-start(s8[8388608]{0:T(1024)(128)(4,1)} %bitcast.211), calls=%async_computation.10 | async-start | bytes 8388608
  396.4 6.7 %slice-start.1 = ((s8[8388608]{0:T(1024)(128)(4,1)}), s8[4194304]{0:T(1024)(128)(4,1)S(1)}, s32[]{:S(2)}) async-start(s8[8388608]{0:T(1024)(128)(4,1)} %bitcast.211), calls=%async_computation.11 | async-start | bytes 8388608
  445.6 12.2 %copy-start.1 = (bf16[1,128,4096]{2,1,0:T(8,128)(2,1)S(1)}, bf16[1,128,4096]{2,1,0:T(8,128)(2,1)}, u32[]{:S(2)}) copy-start(bf16[1,128,4096]{2,1,0:T(8,128)(2,1)} %param.10) | copy-start | bytes 3145732
Sparse Core Ops, SparseCore 0:
  10.2 106.2 all-gather.2
  118.6 77.9 all-gather.4
  407.2 20.8 reduce-scatter.1
where the time goes:
time: 473 us; the launch traced here: 465 us
  waiting for transfers between devices  173 us (37%)
  blocking collectives  95.7 us (20%)
  local copies, waits for them, and re-layouts  68.6 us (15%)
  other arithmetic  51.5 us (11%)
  matrix products  31.7 us (7%)
  starting transfers between devices  29.9 us (6%)
  between operations  14.7 us (3%)
    all_to_all x1, blocking collectives, local(): lax.all_to_all(send_query, 'dp', split_axis=0, concat_axis=0, tiled=True)  95.7 us
    all_gather x1, waiting for transfers between devices, local(): value_full = lax.all_gather(w_value, 'dp', axis=0, tiled=True)  57.3 us
    all_to_all x1, waiting for transfers between devices, local(): lax.all_to_all(send_grad.astype(jnp.float32), 'dp', split_axis=0, concat_...  46.6 us
    all_to_all x1, waiting for transfers between devices, local(): lax.all_to_all(item_part.astype(jnp.float32), 'dp', split_axis=0, concat_...  36.4 us
    unnamed x55, local copies, waits for them, and re-layouts  35.3 us
    all_to_all x1, waiting for transfers between devices, local(): lax.all_to_all(item_dq, 'dp', split_axis=0, concat_axis=0, tiled=True)  31 us
    unnamed x4, other arithmetic  19.7 us
  transfers between devices with their start and end apart: 8, of which 4 were waited for; matrix products, arithmetic and copies ran while one was open for 23% of the time, Pallas kernels for 0%

commit v1 on v0

v1 whole, which is shorter than its diff:
```python
import functools
import math

import jax
import jax.numpy as jnp
from jax import lax
from jax.experimental import pallas as pl
from jax.experimental.pallas import tpu as pltpu
from jax.sharding import PartitionSpec as P

HEAD = 128
CHUNKS = 2
GROUP = 2
F32 = jnp.float32
BF16 = jnp.bfloat16
NT = (((1,), (1,)), ((), ()))
TN = (((0,), (0,)), ((), ()))


def ring_order(chips):
    ny = 1 << ((chips.bit_length() - 1) // 2)
    nz = chips // ny
    order = [z * ny for z in range(nz)]
    for z in reversed(range(nz)):
        columns = range(1, ny) if (nz - 1 - z) % 2 == 0 else reversed(range(1, ny))
        order += [z * ny + y for y in columns]
    return order


class Ring:
    def __init__(self, chips):
        self.chips = chips
        self.order = ring_order(self.chips)
        self.position = [self.order.index(c) for c in range(self.chips)]
        n = self.chips
        pairs = [(self.order[q], self.order[(q + 1) % n]) for q in range(n)]
        self.up = pairs
        self.down = [(b, a) for a, b in pairs]

    def cw(self, x):
        return lax.ppermute(x, "chip", self.up)

    def ccw(self, x):
        return lax.ppermute(x, "chip", self.down)

    def other(self, x):
        return lax.ppermute(x, "core", [(0, 1), (1, 0)])

    def reach(self, flip):
        half = self.chips // 2
        return (half - 1, half) if flip else (half, half - 1)

    def gather(self, own, flip):
        n = self.chips
        ups, downs = self.reach(flip)
        out = [own] + [None] * (n - 1)
        up = down = own
        for s in range(1, max(ups, downs) + 1):
            if s <= ups:
                out[s] = up = self.cw(up)
            if s <= downs:
                out[n - s] = down = self.ccw(down)
        return out

    def reduce(self, part, flip):
        n = self.chips
        ups, downs = self.reach(flip)
        up = down = None

        def plus(a, b):
            return a if b is None else (a.astype(F32) + b.astype(F32)).astype(BF16)

        for s in range(max(ups, downs), 0, -1):
            if s <= ups:
                up = self.cw(plus(part[n - s], up))
            if s <= downs:
                down = self.ccw(plus(part[s], down))
        return part[0], up, down


def after(x, *others, cost=1):
    hbm = pl.BlockSpec(memory_space=pl.ANY)
    return pl.pallas_call(
        lambda *refs: None,
        out_shape=jax.ShapeDtypeStruct(x.shape, x.dtype),
        in_specs=[hbm] * (1 + len(others)),
        out_specs=hbm,
        input_output_aliases={0: 0},
        cost_estimate=pl.CostEstimate(flops=cost, bytes_accessed=1, transcendentals=0),
        name="after",
    )(x, *others)


def room(*shapes):
    return sum(math.prod(shape) * size for shape, size in shapes) + 8 * 1024 * 1024


def pieces(refs, depth):
    return [ref.at[pl.ds(i, depth)] for ref in refs for i in range(0, ref.shape[0], depth)]


def rows_kernel(count, depth, has_before, cuts, feature_ref, low_ref, high_ref, *refs):
    weights, refs = refs[:count], refs[count:]
    if has_before:
        before, refs = refs[0], refs[1:]
    outs, (held, sems) = refs[:cuts], refs[cuts:]
    views = pieces(weights, depth)
    copies = []
    for p, view in enumerate(views):
        copies.append(pltpu.make_async_copy(view, held.at[pl.ds(p * depth, depth)], sems.at[p]))
        copies[-1].start()
    wide = depth if depth % 128 == 0 else 2 * depth
    left = []
    for p in range(0, len(views), wide // depth):
        at = pl.ds(pl.multiple_of(feature_ref[p], wide), wide)
        left.append(jnp.concatenate([low_ref[:, at], high_ref[:, at]], axis=0))
    left = jnp.concatenate(left, axis=1)
    for copy in copies:
        copy.wait()
    total = jnp.dot(left, held[...], preferred_element_type=F32)
    if has_before:
        total += before[...]
    columns = outs[0].shape[1]
    for i, out in enumerate(outs):
        out[...] = total[:, i * columns : (i + 1) * columns].astype(out.dtype)


def add_rows(features, low, high, depth, weights, before, cuts):
    flat = [w for block in weights for w in block]
    tokens = low.shape[0]
    width = flat[0].shape[1]
    held = sum(w.shape[0] for w in flat)
    vmem = pl.BlockSpec(memory_space=pltpu.VMEM)
    earlier = [] if before is None else [before]
    outs = max(cuts, 1)
    out = jax.ShapeDtypeStruct((2 * tokens, width // outs), BF16 if cuts else F32)
    result = pl.pallas_call(
        functools.partial(rows_kernel, len(flat), depth, before is not None, outs),
        out_shape=[out] * outs,
        in_specs=[pl.BlockSpec(memory_space=pltpu.SMEM), vmem, vmem]
        + [pl.BlockSpec(memory_space=pl.ANY)] * len(flat)
        + [vmem] * len(earlier),
        out_specs=[vmem] * outs,
        scratch_shapes=[
            pltpu.VMEM((held, width), BF16),
            pltpu.SemaphoreType.DMA((held // depth,)),
        ],
        compiler_params=pltpu.CompilerParams(
            vmem_limit_bytes=room(
                (low.shape, 4), ((held, width), 2), ((2 * tokens, held), 2), ((2 * tokens, width), 12)
            )
        ),
        cost_estimate=pl.CostEstimate(
            flops=12 * tokens * held * width, bytes_accessed=2 * held * width, transcendentals=0
        ),
        name="rows",
    )(features, low, high, *flat, *earlier)
    return result if cuts else result[0]


PARTS = 4


def state_kernel(chunks, count, depth, dmodel, offset, info_ref, *refs):
    sums, weights, refs = refs[: 3 * chunks], refs[3 * chunks : 3 * chunks + count], refs[3 * chunks + count :]
    out_mine, out_pair, right, held, sems = refs
    tokens = right.shape[1] // 2
    features = held.shape[0]
    part = features // PARTS
    for p, view in enumerate(pieces(weights, depth)):
        to = lax.rem(info_ref[2 + p] - info_ref[0] + dmodel, dmodel) - offset

        @pl.when((to >= 0) & (to < features))
        def _(view=view, to=to):
            pltpu.make_async_copy(
                view, held.at[pl.ds(pl.multiple_of(to, depth), depth)], sems.at[lax.div(to, part)]
            ).start()

    width = sums[0].shape[1]
    for k in range(chunks):
        own, up, down = (sums[3 * k + j][...].astype(F32) for j in range(3))
        right[k * width : (k + 1) * width, :] = (own + up + down).astype(BF16).T
    second = info_ref[1] == 1
    for b in range(PARTS):
        at = slice(b * part, (b + 1) * part)
        block = held.at[pl.ds(b * part, part)]
        pltpu.make_async_copy(block, block, sems.at[b]).wait()
        total = jnp.dot(held[at, :], right[...], preferred_element_type=F32)
        low, high = total[:, :tokens], total[:, tokens:]
        out_mine[at, :] = jnp.where(second, high, low)
        out_pair[at, :] = jnp.where(second, low, high).astype(BF16)


def state_terms(info, offset, features, depth, dmodel, sums, weights):
    flat_sums = [x for group in sums for x in group]
    flat = [w for block in weights for w in block]
    tokens = flat_sums[0].shape[0]
    width = flat[0].shape[1]
    vmem, hbm = pl.BlockSpec(memory_space=pltpu.VMEM), pl.BlockSpec(memory_space=pl.ANY)
    return pl.pallas_call(
        functools.partial(state_kernel, len(sums), len(flat), depth, dmodel, offset),
        out_shape=[
            jax.ShapeDtypeStruct((features, tokens // 2), F32),
            jax.ShapeDtypeStruct((features, tokens // 2), BF16),
        ],
        in_specs=[pl.BlockSpec(memory_space=pltpu.SMEM)]
        + [vmem] * len(flat_sums)
        + [hbm] * len(flat),
        out_specs=[vmem, vmem],
        scratch_shapes=[
            pltpu.VMEM((width, tokens), BF16),
            pltpu.VMEM((features, width), BF16),
            pltpu.SemaphoreType.DMA((PARTS,)),
        ],
        compiler_params=pltpu.CompilerParams(
            vmem_limit_bytes=60 * 1024 * 1024
        ),
        cost_estimate=pl.CostEstimate(flops=1, bytes_accessed=1, transcendentals=0),
        name="state",
    )(info, *flat_sums, *flat)


def final_kernel(own_ref, got_ref, out_ref):
    out_ref[...] = (own_ref[...].astype(F32) + got_ref[...].astype(F32)).T.astype(BF16)


def finish(own, got):
    features, tokens = own.shape
    block = features // PARTS
    part = pl.BlockSpec((block, tokens), lambda i: (i, 0))
    return pl.pallas_call(
        final_kernel,
        out_shape=jax.ShapeDtypeStruct((tokens, features), BF16),
        grid=(PARTS,),
        in_specs=[part, part],
        out_specs=pl.BlockSpec((tokens, block), lambda i: (0, i)),
        compiler_params=pltpu.CompilerParams(vmem_limit_bytes=60 * 1024 * 1024),
        cost_estimate=pl.CostEstimate(
            flops=2 * own.size, bytes_accessed=6 * own.size, transcendentals=0
        ),
        name="finish",
    )(own, got)


def attend_kernel(blocks, heads, spans, neigh, offset, slot_ref, count_ref, *refs):
    tokens_hbm, rows_hbm, refs = refs[:4], refs[4 : 4 + blocks], refs[4 + blocks :]
    contexts, query_grads, grads = refs[0:2], refs[2:4], refs[4 : 4 + blocks]
    tokens, rows, total, sems = refs[4 + blocks :]
    width = heads * HEAD
    span_len = tokens.shape[1] // spans
    scale = 1.0 / math.sqrt(HEAD)
    length = rows.shape[1]
    copies = []
    for i, ref in enumerate(tokens_hbm):
        first = offset + (0 if i % 2 else slot_ref[slot_ref.shape[0] - 1])
        view = ref.at[:, pl.ds(pl.multiple_of(first, HEAD), width)]
        copies.append(pltpu.make_async_copy(view, tokens.at[i], sems.at[i]))
    for b in range(2 * blocks):
        view = rows_hbm[b // 2].at[pl.ds(b % 2 * length, length)]
        copies.append(pltpu.make_async_copy(view, rows.at[b], sems.at[4 + b]))
    for copy in copies:
        copy.start()
    queries, cotangents = [tokens.at[0], tokens.at[1]], [tokens.at[2], tokens.at[3]]
    total[...] = jnp.zeros_like(total)
    for copy in copies:
        copy.wait()

    def together(first, sides):
        chains = [
            (side, first + u, g) for u in range(GROUP) for side in sides for g in range(heads)
        ]
        at = [pl.ds(pl.multiple_of(span * span_len, span_len), span_len) for _, span, _ in chains]
        index = {
            (h, j): slot_ref[(side * spans + span) * neigh + j]
            for h, (side, span, _) in enumerate(chains)
            for j in range(neigh)
        }
        live = [
            [j < count_ref[side * spans + span] for j in range(neigh)] for side, span, _ in chains
        ]
        kcols = [slice(g * HEAD, (g + 1) * HEAD) for _, _, g in chains]
        vcols = [slice(width + g * HEAD, width + (g + 1) * HEAD) for _, _, g in chains]
        items = [(h, j) for h in range(len(chains)) for j in range(neigh)]
        query = [queries[chains[h][0]][at[h], c] for h, c in enumerate(kcols)]
        keys = {(h, j): rows[index[h, j], :, kcols[h]] for h, j in items}
        def diagonal(left, right, product, axis):
            out = {}
            for h in range(len(chains)):
                both = product(
                    jnp.concatenate([left[h, j] for j in range(neigh)]),
                    jnp.concatenate([right[h, j] for j in range(neigh)], axis=axis),
                    preferred_element_type=F32,
                )
                for j in range(neigh):
                    at = slice(j * span_len, (j + 1) * span_len)
                    out[h, j] = both[at, j * HEAD : (j + 1) * HEAD]
            return out

        length = rows.shape[1]
        joint = [jnp.concatenate([keys[h, j] for j in range(neigh)]) for h in range(len(chains))]
        joint = [
            lax.dot_general(query[h], joint[h], NT, preferred_element_type=F32)
            for h in range(len(chains))
        ]
        score = {(h, j): joint[h][:, j * length : (j + 1) * length] * scale for h, j in items}
        top = {i: jnp.max(score[i], axis=1, keepdims=True) for i in items}
        powers = {i: jnp.exp(score[i] - top[i]) for i in items}
        norm = {i: jnp.sum(powers[i], axis=1, keepdims=True) for i in items}
        prob = {i: powers[i] * (1.0 / norm[i]) for i in items}
        half = {i: prob[i].astype(BF16) for i in items}
        values = {(h, j): rows[index[h, j], :, vcols[h]] for h, j in items}
        part = {
            i: x.astype(BF16).astype(F32) for i, x in diagonal(half, values, jnp.dot, 1).items()
        }
        log_total = {i: top[i] + jnp.log(norm[i]) for i in items}
        mix, mixed = {}, {}
        for h in range(len(chains)):
            masked = [jnp.where(live[h][j], log_total[h, j], -1e30) for j in range(neigh)]
            best = functools.reduce(jnp.maximum, masked)
            raw = [jnp.where(live[h][j], jnp.exp(masked[j] - best), 0.0) for j in range(neigh)]
            below = 1.0 / functools.reduce(jnp.add, raw)
            for j in range(neigh):
                mix[h, j] = raw[j] * below
        cot = [cotangents[chains[h][0]][at[h], c].astype(F32) for h, c in enumerate(kcols)]
        exact = {(h, j): mix[h, j] * cot[h] for h, j in items}
        pgrad = {i: exact[i].astype(BF16) for i in items}
        dprob = diagonal(pgrad, values, functools.partial(lax.dot_general, dimension_numbers=NT), 0)
        for h in range(len(chains)):
            mixed[h] = functools.reduce(jnp.add, [mix[h, j] * part[h, j] for j in range(neigh)])
        rest_term = {
            (h, j): jnp.sum(
                (pgrad[h, j].astype(F32) - exact[h, j]) * part[h, j] + exact[h, j] * mixed[h],
                axis=1,
                keepdims=True,
            )
            for h, j in items
        }
        dscore = {i: (prob[i] * (dprob[i] - rest_term[i])).astype(BF16) for i in items}
        slot_dq = {
            i: (x * scale).astype(BF16).astype(F32)
            for i, x in diagonal(dscore, keys, jnp.dot, 1).items()
        }
        joint = [
            jnp.concatenate([dscore[h, j] for j in range(neigh)], axis=1)
            for h in range(len(chains))
        ]
        joint = [
            lax.dot_general(joint[h], query[h], TN, preferred_element_type=F32)
            for h in range(len(chains))
        ]
        dkey = {(h, j): joint[h][j * length : (j + 1) * length] for h, j in items}
        dvalue = {
            i: lax.dot_general(half[i], pgrad[i], TN, preferred_element_type=F32) for i in items
        }
        for h in range(len(chains)):
            contexts[chains[h][0]][at[h], kcols[h]] = mixed[h].astype(BF16)
            dquery = functools.reduce(jnp.add, [slot_dq[h, j] for j in range(neigh)])
            query_grads[chains[h][0]][at[h], kcols[h]] = dquery.astype(BF16)
        for h, j in items:
            total[index[h, j], :, kcols[h]] += dkey[h, j]
            total[index[h, j], :, vcols[h]] += dvalue[h, j]

    for sides in [(0, 1)] if heads <= 2 else [(0,), (1,)]:

        @pl.loop(0, spans // GROUP)
        def _(step):
            together(step * GROUP, sides)

    for b in range(rows.shape[0]):
        out, first = divmod(b * length, grads[0].shape[0])
        to = slice(first, first + length)
        grads[out][to, :width] = (total[b, :, :width] * scale).astype(BF16)
        grads[out][to, width:] = total[b, :, width:].astype(BF16)


def attend(slots, counts, tokens, rows, offset, spans, neigh):
    blocks = len(rows)
    count = tokens[0].shape[0]
    width = rows[0].shape[1] // 2
    heads = width // HEAD
    length = rows[0].shape[0] // 2
    span_len = count // spans
    vmem, hbm = pl.BlockSpec(memory_space=pltpu.VMEM), pl.BlockSpec(memory_space=pl.ANY)
    smem = pl.BlockSpec(memory_space=pltpu.SMEM)
    tok = jax.ShapeDtypeStruct((count, width), BF16)
    grad = jax.ShapeDtypeStruct((2 * length, 2 * width), BF16)
    work = 2 * spans * neigh * heads * span_len * length * HEAD * 2
    out = pl.pallas_call(
        functools.partial(attend_kernel, blocks, heads, spans, neigh, offset),
        out_shape=[tok] * 4 + [grad] * blocks,
        in_specs=[smem, smem] + [hbm] * (4 + blocks),
        out_specs=[vmem] * (4 + blocks),
        scratch_shapes=[
            pltpu.VMEM((4, count, width), BF16),
            pltpu.VMEM((2 * blocks, length, 2 * width), BF16),
            pltpu.VMEM((2 * blocks, length, 2 * width), F32),
            pltpu.SemaphoreType.DMA((4 + 2 * blocks,)),
        ],
        compiler_params=pltpu.CompilerParams(vmem_limit_bytes=60 * 1024 * 1024),
        cost_estimate=pl.CostEstimate(
            flops=20 * work,
            bytes_accessed=2 * blocks * length * width * 8,
            transcendentals=2 * spans * neigh * heads * span_len * length,
        ),
        name="attend",
    )(slots, counts, *tokens, *rows)
    return out[0:2], out[2:4], out[4:]


def columns_of(x, first, size):
    return lax.dynamic_slice_in_dim(x, first, size, axis=1)


def both_ways(core, mine, other):
    swapped = core == 1
    return jnp.concatenate([jnp.where(swapped, other, mine), jnp.where(swapped, mine, other)], axis=1)


def local(queries, neighbours, counts, states, w_key, w_value, cotangent):
    ring = Ring(lax.axis_size("chip"))
    chips = ring.chips
    chip, core = lax.axis_index("chip"), lax.axis_index("core")
    tensors, across = lax.axis_size("tensor"), lax.axis_index("tensor")
    place = jnp.asarray(ring.position, jnp.int32)
    here = place[chip]
    spans, neigh = neighbours.shape
    length, dmodel = states.shape[1:]
    half = queries.shape[1] // 2
    heads = half // HEAD
    chunks = min(CHUNKS, heads) if chips <= 8 else 1
    width = half // chunks
    first_mine, first_other = core * half, (1 - core) * half

    swapped = core == 1
    depth = w_key.shape[0]

    def in_order(mine, came):
        return jnp.where(swapped, came, mine), jnp.where(swapped, mine, came)

    keep, send = (
        jnp.concatenate(
            [
                columns_of(w, first + k * width, width)
                for k in range(chunks)
                for w in (w_key, w_value)
            ],
            axis=1,
        )
        for first in (first_mine, first_other)
    )
    shard = [keep, ring.other(send)]
    if depth % 128:
        shard = in_order(*shard)
    weights = [list(block) for block in zip(*(ring.gather(x, j) for j, x in enumerate(shard)))]
    mine_states = states.reshape(length, dmodel)
    low, high = in_order(mine_states, ring.other(mine_states))
    small = jnp.concatenate([neighbours, counts[:, None]], axis=1)
    small = jnp.stack([small, ring.other(small)])
    ids = small[:, :, :neigh].reshape(2 * spans * neigh)
    live_counts = small[:, :, neigh].reshape(2 * spans)
    slots = 2 * ((here - place[ids // 2]) % chips) + ids % 2
    behind = jnp.asarray(ring.order, jnp.int32)[(here - jnp.arange(chips, dtype=jnp.int32)) % chips]
    cores = jnp.arange(2, dtype=jnp.int32)
    if depth % 128 == 0:
        cores = cores ^ core
    features = (2 * behind[:, None] + cores[None, :]) * depth
    slots = jnp.concatenate([slots, first_mine[None]])
    tokens = [
        y for x in (queries, cotangent) for y in (x, ring.other(columns_of(x, first_other, half)))
    ]

    wide = dmodel // tensors
    info = jnp.concatenate([jnp.stack([(across + 1) % tensors * wide, core]), features.reshape(-1)])
    early = [r for r in range(chips) if min(r, chips - r) <= chips // 2 - 2]
    late = [r for r in range(chips) if r not in early]
    total = None
    for group in (early, late):
        where = jnp.stack([features[r] for r in group]).reshape(-1)
        picked = [weights[r] for r in group]
        total = add_rows(where, low, high, depth, picked, total, chunks if group is late else 0)
    context, query_grad, sums, rows = [], [], [], None
    for k in range(chunks):
        own = total[k]
        if k:
            ahead = min(2, chips // 2 - 1)
            own = after(own, rows[ahead], rows[chips - ahead])
        rows = ring.gather(own, k % 2)
        ctx, dq, parts = attend(slots, live_counts, tokens, rows, k * width, spans, neigh)
        context.append(ctx)
        query_grad.append(dq)
        sums.append(ring.reduce(parts, k % 2))
    swap_out = []
    for group in (context, query_grad):
        keep = jnp.concatenate([g[0] for g in group], axis=1)
        send = jnp.concatenate([g[1] for g in group], axis=1)
        swap_out.append(both_ways(core, keep, ring.other(send)))
    sums[0] = (after(sums[0][0], *swap_out),) + sums[0][1:]
    got = None
    for s in range(1, tensors + 1):
        ends = list(sums)
        if s > 1:
            ends[0] = (after(ends[0][0], term),) + tuple(ends[0][1:])
        term_mine, term_pair = state_terms(
            info, (s - 1) * wide, wide, depth, dmodel, ends, weights
        )
        term = (term_mine + ring.other(term_pair).astype(F32)).astype(BF16)
        if s < tensors:
            went = lax.ppermute(term, "tensor", [(i, (i + s) % tensors) for i in range(tensors)])
            got = went if got is None else got.astype(F32) + went.astype(F32)
    final = finish(term, after(got, cost=20_000_000_000))
    return swap_out[0], swap_out[1], final.reshape((1,) + final.shape)


def solution(mesh):
    devices = mesh.devices
    shape = (devices.shape[0] // 2, 2, devices.shape[1])
    by_chip = jax.sharding.Mesh(devices.reshape(shape), ("chip", "core", "tensor"))
    dp = ("chip", "core")
    placed = (
        P(dp, "tensor"),
        P(dp, None),
        P(dp),
        P(dp, None, None),
        P(dp, "tensor"),
        P(dp, "tensor"),
        P(dp, "tensor"),
    )
    return jax.shard_map(
        local,
        mesh=by_chip,
        in_specs=placed,
        out_specs=(P(dp, "tensor"), P(dp, "tensor"), P(dp, None, "tensor")),
        check_vma=False,
    )
```

time: 473 us -> 228 us (0.48)
  blocking collectives: 95.7 us -> 0 us
  waiting for transfers between devices: 173 us -> 102 us
  local copies, waits for them, and re-layouts: 68.6 us -> 10.7 us
  Pallas kernels: 0 us -> 45.5 us
  other arithmetic: 51.5 us -> 9.67 us
  matrix products: 31.7 us -> 0 us
  starting transfers between devices: 29.9 us -> 54.1 us
  between operations: 14.7 us -> 1.38 us
    all_to_all x5 -> x0, waiting for transfers between devices: 114 us -> none  [the longest x1 46.6 us: local(): lax.all_to_all(send_grad.astype(jnp.float32), 'dp', split_axis=0, concat_...]
    ppermute x0 -> x52, waiting for transfers between devices: none -> 102 us  [the longest x21 52.7 us: ccw(): return lax.ppermute(x, 'chip', self.down)]
    all_to_all x1 -> x0, blocking collectives: 95.7 us -> none  [local(): lax.all_to_all(send_query, 'dp', split_axis=0, concat_axis=0, tiled=True)]
    all_gather x2 -> x0, waiting for transfers between devices: 57.4 us -> none  [the longest x1 57.3 us: local(): value_full = lax.all_gather(w_value, 'dp', axis=0, tiled=True)]
    ppermute x0 -> x52, starting transfers between devices: none -> 54.1 us  [the longest x21 29.4 us: ccw(): return lax.ppermute(x, 'chip', self.down)]
    pallas_call x0 -> x11, Pallas kernels: none -> 45.5 us  [the longest x2 20.8 us: attend(): pl.pallas_call(functools.partial(attend_kernel, blocks, heads, spans, nei...]
    all_to_all x5 -> x0, starting transfers between devices: 29.8 us -> none  [the longest x1 7.66 us: local(): lax.all_to_all(log_total, 'dp', split_axis=0, concat_axis=0, tiled=True)]
    unnamed x55 -> x110, local copies, waits for them, and re-layouts: 35.3 us -> 5.78 us
  transfers between devices with their start and end apart: 8 -> 52, of which waited for: 4 -> 26; matrix products, arithmetic and copies ran while one was open for 23% -> 6% of each run, Pallas kernels for 0% -> 14%
where the time goes in v1:
time: 228 us; the launch traced here: 224 us
  waiting for transfers between devices  102 us (45%)
  starting transfers between devices  54.1 us (24%)
  Pallas kernels  45.5 us (20%)
  local copies, waits for them, and re-layouts  10.7 us (5%)
  other arithmetic  9.67 us (4%)
    ppermute x21, waiting for transfers between devices, ccw(): return lax.ppermute(x, 'chip', self.down)  52.7 us
    ppermute x21, waiting for transfers between devices, cw(): return lax.ppermute(x, 'chip', self.up)  42.4 us
    ppermute x21, starting transfers between devices, ccw(): return lax.ppermute(x, 'chip', self.down)  29.4 us
    pallas_call x2, Pallas kernels, attend(): pl.pallas_call(functools.partial(attend_kernel, blocks, heads, spans, nei...  20.8 us
    ppermute x9, starting transfers between devices, other(): return lax.ppermute(x, 'core', [(0, 1), (1, 0)])  19.9 us
    pallas_call x2, Pallas kernels, state_terms(): pl.pallas_call(functools.partial(state_kernel, len(sums), len(flat), dept...  14.6 us
    pallas_call x2, Pallas kernels, add_rows(): pl.pallas_call(functools.partial(rows_kernel, len(flat), depth, before is...  6.63 us
    unnamed x110, local copies, waits for them, and re-layouts  5.78 us
  transfers between devices with their start and end apart: 52, of which 26 were waited for; matrix products, arithmetic and copies ran while one was open for 6% of the time, Pallas kernels for 14%

profile of v1, /device:TPU:13, one launch (start us, length us, event | category | flops | bytes accessed | tf_op | source)
XLA Modules:
  0.0 223.9 jit_solution(8207151201048743425)
XLA Ops:
  0.6 1.4 constant_dynamic-slice_fusion.2
  5.7 1.3 collective-permute-start.16
  8.7 7.9 %collective-permute-done.4.refs_2_.refs_8_ = bf16[256,1024]{1,0:T(8,128)(2,1)S(1)} collective-permute-done((bf16[256,1024]{1,0:T(8,128)(2,1)S(1)}, bf16[256,1024]{1,0:T(8,128)(2,1)S(1)}, u32[]{:S(2)}, u32[]{:S(2)}) %collective-permute-start.4) | collective-permute-done | bytes 524320 | tf_op jit(solution)/shard_map/ppermute | solution.py:41
  20.1 8.8 %collective-permute-done.16.refs_8_.refs_20_ = bf16[256,1024]{1,0:T(8,128)(2,1)S(1)} collective-permute-done((bf16[256,1024]{1,0:T(8,128)(2,1)S(1)}, bf16[256,1024]{1,0:T(8,128)(2,1)S(1)}, u32[]{:S(2)}, u32[]{:S(2)}) %collective-permute-start.16) | collective-permute-done | bytes 524320 | tf_op jit(solution)/shard_map/ppermute | solution.py:44
  28.9 1.3 collective-permute-start.17
  30.3 8.7 %collective-permute-done.5.refs_4_.refs_10_ = bf16[256,1024]{1,0:T(8,128)(2,1)} collective-permute-done((bf16[256,1024]{1,0:T(8,128)(2,1)S(1)}, bf16[256,1024]{1,0:T(8,128)(2,1)}, u32[]{:S(2)}, u32[]{:S(2)}) %collective-permute-start.5) | collective-permute-done | bytes 524320 | tf_op jit(solution)/shard_map/ppermute | solution.py:41
  40.1 1.3 collective-permute-start.14
  42.0 9.3 %collective-permute-done.17.refs_6_.refs_18_ = bf16[256,1024]{1,0:T(8,128)(2,1)} collective-permute-done((bf16[256,1024]{1,0:T(8,128)(2,1)S(1)}, bf16[256,1024]{1,0:T(8,128)(2,1)}, u32[]{:S(2)}, u32[]{:S(2)}) %collective-permute-start.17) | collective-permute-done | bytes 524320 | tf_op jit(solution)/shard_map/ppermute | solution.py:44
  52.8 8.8 %collective-permute-done.6.refs_0_.refs_12_ = bf16[256,1024]{1,0:T(8,128)(2,1)} collective-permute-done((bf16[256,1024]{1,0:T(8,128)(2,1)}, bf16[256,1024]{1,0:T(8,128)(2,1)}, u32[]{:S(2)}, u32[]{:S(2)}) %collective-permute-start.6) | collective-permute-done | bytes 524320 | tf_op jit(solution)/shard_map/ppermute | solution.py:41
  63.9 1.7 broadcast_select_fusion
  65.6 3.8 %rows.2.refs_6_ = f32[256,1024]{1,0:T(8,128)S(1)} custom-call(s32[10]{0:T(128)S(1)} %reshape.169.feature_ref, bf16[128,4096]{1,0:T(8,128)(2,1)S(1)} %get-tuple-element.64.low_ref, bf16[128,4096]{1,0:T(8,128)(2,1)S(1)} %get-tuple-element.63.high_ref, bf16[256,1024]{1,0:T(8,128)(2,1)S(1)} %pad_maximum_fusion.2.refs_0_.refs_6_, ...), custom_call_target="tpu_custom_call" | custom-call | flops 4026531840 | bytes 5242880 | tf_op jit(solution)/shard_map/rows/pallas_call | solution.py:137
  69.5 4.2 %collective-permute-done.18.refs_4_.refs_16_ = bf16[256,1024]{1,0:T(8,128)(2,1)S(1)} collective-permute-done((bf16[256,1024]{1,0:T(8,128)(2,1)}, bf16[256,1024]{1,0:T(8,128)(2,1)S(1)}, u32[]{:S(2)}, u32[]{:S(2)}) %collective-permute-start.18) | collective-permute-done | bytes 524320 | tf_op jit(solution)/shard_map/ppermute | solution.py:44
  73.7 10.2 %collective-permute-done.11.refs_2_.refs_14_ = bf16[256,1024]{1,0:T(8,128)(2,1)S(1)} collective-permute-done((bf16[256,1024]{1,0:T(8,128)(2,1)}, bf16[256,1024]{1,0:T(8,128)(2,1)S(1)}, u32[]{:S(2)}, u32[]{:S(2)}) %collective-permute-start.11) | collective-permute-done | bytes 524320 | tf_op jit(solution)/shard_map/ppermute | solution.py:41
  84.9 2.8 %rows.3 = (bf16[256,512]{1,0:T(8,128)(2,1)S(1)}, bf16[256,512]{1,0:T(8,128)(2,1)S(1)}) custom-call(s32[6]{0:T(128)S(1)} %reshape.167.feature_ref, bf16[128,4096]{1,0:T(8,128)(2,1)S(1)} %get-tuple-element.64.low_ref, bf16[128,4096]{1,0:T(8,128)(2,1)S(1)} %get-tuple-element.63.high_ref, bf16[256,1024]{1,0:T(8,128)(2,1)} %collective-permute-done.6.refs_0_.refs_12_, ...), custom_call_target="tpu_custom_call" | custom-call | flops 2415919104 | bytes 3145728 | tf_op jit(solution)/shard_map/rows/pallas_call | solution.py:137
  89.4 1.8 collective-permute-start
  91.2 3.3 %collective-permute-done.19.refs_5_ = bf16[256,512]{1,0:T(8,128)(2,1)S(1)} collective-permute-done((bf16[256,512]{1,0:T(8,128)(2,1)S(1)}, bf16[256,512]{1,0:T(8,128)(2,1)S(1)}, u32[]{:S(2)}, u32[]{:S(2)}) %collective-permute-start.19) | collective-permute-done | bytes 262176 | tf_op jit(solution)/shard_map/ppermute | solution.py:41
  94.7 2.5 %collective-permute-start.1 = (bf16[512,512]{1,0:T(8,128)(2,1)S(1)}, bf16[512,512]{1,0:T(8,128)(2,1)S(1)}, u32[]{:S(2)}, u32[]{:S(2)}) collective-permute-start(bf16[512,512]{1,0:T(8,128)(2,1)S(1)} %constant_dynamic-slice_fusion.9), channel_id=1, source_target_pairs={{0,2},{2,0},{1,3},{3,1},{4,6},{6,4},{5,7},{7,5},{8,10},{10,8},{9,1... | collective-permute-start | bytes 1572872 | tf_op jit(solution)/shard_map/ppermute | solution.py:47
  97.5 1.3 collective-permute-start.24
  100.4 4.6 %collective-permute-done.24.refs_10_.refs_2_ = bf16[256,512]{1,0:T(8,128)(2,1)S(1)} collective-permute-done((bf16[256,512]{1,0:T(8,128)(2,1)S(1)}, bf16[256,512]{1,0:T(8,128)(2,1)S(1)}, u32[]{:S(2)}, u32[]{:S(2)}) %collective-permute-start.24) | collective-permute-done | bytes 262176 | tf_op jit(solution)/shard_map/ppermute | solution.py:44
  105.7 1.3 collective-permute-start.29
  108.0 1.3 collective-permute-start.25
  110.0 2.3 %collective-permute-done.29.refs_11_ = bf16[256,512]{1,0:T(8,128)(2,1)S(1)} collective-permute-done((bf16[256,512]{1,0:T(8,128)(2,1)}, bf16[256,512]{1,0:T(8,128)(2,1)S(1)}, u32[]{:S(2)}, u32[]{:S(2)}) %collective-permute-start.29) | collective-permute-done | bytes 262176 | tf_op jit(solution)/shard_map/ppermute | solution.py:44
  112.4 1.3 collective-permute-start.30
  115.1 3.0 %collective-permute-done.25.refs_9_ = bf16[256,512]{1,0:T(8,128)(2,1)S(1)} collective-permute-done((bf16[256,512]{1,0:T(8,128)(2,1)}, bf16[256,512]{1,0:T(8,128)(2,1)S(1)}, u32[]{:S(2)}, u32[]{:S(2)}) %collective-permute-start.25) | collective-permute-done | bytes 262176 | tf_op jit(solution)/shard_map/ppermute | solution.py:44
  118.1 1.7 collective-permute-done.22.refs_8_
  120.5 10.4 %attend.2 = (bf16[512,256]{1,0:T(8,128)(2,1)}, bf16[512,256]{1,0:T(8,128)(2,1)}, bf16[512,256]{1,0:T(8,128)(2,1)}, bf16[512,256]{1,0:T(8,128)(2,1)}, bf16[256,51...) custom-call(s32[33]{0:T(128)} %pad_add_fusion.3.slot_ref, ...), custom_call_target="tpu_custom_call" | custom-call | flops 2684354560 | bytes 4194304 | tf_op jit(solution)/shard_map/attend/pallas_call | solution.py:388
  131.0 1.4 collective-permute-start.39
  136.6 3.4 %collective-permute-done.31.refs_9_ = bf16[256,512]{1,0:T(8,128)(2,1)S(1)} collective-permute-done((bf16[256,512]{1,0:T(8,128)(2,1)S(1)}, bf16[256,512]{1,0:T(8,128)(2,1)S(1)}, u32[]{:S(2)}, u32[]{:S(2)}) %collective-permute-start.31) | collective-permute-done | bytes 262176 | tf_op jit(solution)/shard_map/ppermute | solution.py:44
  139.9 1.3 collective-permute-start.32
  141.3 1.3 collective-permute-start.40
  143.0 5.0 %collective-permute-done.32.refs_8_ = bf16[256,512]{1,0:T(8,128)(2,1)S(1)} collective-permute-done((bf16[256,512]{1,0:T(8,128)(2,1)S(1)}, bf16[256,512]{1,0:T(8,128)(2,1)S(1)}, u32[]{:S(2)}, u32[]{:S(2)}) %collective-permute-start.32) | collective-permute-done | bytes 262176 | tf_op jit(solution)/shard_map/ppermute | solution.py:44
  148.7 10.4 %attend.3 = (bf16[512,256]{1,0:T(8,128)(2,1)}, bf16[512,256]{1,0:T(8,128)(2,1)}, bf16[512,256]{1,0:T(8,128)(2,1)}, bf16[512,256]{1,0:T(8,128)(2,1)}, bf16[256,51...) custom-call(s32[33]{0:T(128)} %pad_add_fusion.3.slot_ref, ...), custom_call_target="tpu_custom_call" | custom-call | flops 2684354560 | bytes 4194304 | tf_op jit(solution)/shard_map/attend/pallas_call | solution.py:388
  159.2 1.4 collective-permute-start.45
  160.8 1.5 collective-permute-start.41
  162.7 7.6 %collective-permute-start.34 = (bf16[512,512]{1,0:T(8,128)(2,1)S(1)}, bf16[512,512]{1,0:T(8,128)(2,1)S(1)}, u32[]{:S(2)}, u32[]{:S(2)}) collective-permute-start(bf16[512,512]{1,0:T(8,128)(2,1)S(1)} %pad_maximum_fusion.5), channel_id=1, source_target_pairs={{0,2},{2,0},{1,3},{3,1},{4,6},{6,4},{5,7},{7,5},{8,10},{10,8},{9,1... | collective-permute-start | bytes 1572872 | tf_op jit(solution)/shard_map/ppermute | solution.py:47
  170.4 1.8 collective-permute-start.33
  172.3 1.4 collective-permute-start.46
  174.3 4.4 %collective-permute-done.46 = bf16[256,512]{1,0:T(8,128)(2,1)S(1)} collective-permute-done((bf16[256,512]{1,0:T(8,128)(2,1)S(1)}, bf16[256,512]{1,0:T(8,128)(2,1)S(1)}, u32[]{:S(2)}, u32[]{:S(2)}) %collective-permute-start.46) | collective-permute-done | bytes 262176 | tf_op jit(solution)/shard_map/ppermute | solution.py:44
  178.8 1.6 collective-permute-start.47
  180.6 3.7 %collective-permute-done.47 = bf16[256,512]{1,0:T(8,128)(2,1)S(1)} collective-permute-done((bf16[256,512]{1,0:T(8,128)(2,1)S(1)}, bf16[256,512]{1,0:T(8,128)(2,1)S(1)}, u32[]{:S(2)}, u32[]{:S(2)}) %collective-permute-start.47) | collective-permute-done | bytes 262176 | tf_op jit(solution)/shard_map/ppermute | solution.py:44
  184.4 2.7 %collective-permute-start.48 = (bf16[256,512]{1,0:T(8,128)(2,1)S(1)}, bf16[256,512]{1,0:T(8,128)(2,1)S(1)}, u32[]{:S(2)}, u32[]{:S(2)}) collective-permute-start(bf16[256,512]{1,0:T(8,128)(2,1)S(1)} %add_convert_fusion.2), channel_id=1, source_target_pairs={{8,0},{16,8},{24,16},{28,24},{20,28},{12,20},{4,12},{0,4},{9,1},{1... | collective-permute-start | bytes 786440 | tf_op jit(solution)/shard_map/ppermute | solution.py:44
  191.1 7.5 %state.2 = (f32[2048,128]{1,0:T(8,128)}, bf16[2048,128]{1,0:T(8,128)(2,1)}) custom-call(s32[18]{0:T(128)} %pad_add_fusion.4.info_ref, bf16[256,512]{1,0:T(8,128)(2,1)} %after.5.refs_0_, bf16[256,512]{1,0:T(8,128)(2,1)} %copy-done.16, bf16[256,512]{1,0:T(8,128)(2,1)} %copy-done.15, bf16[256,512]{1,0:T(8,128)(2,1)} %get-tuple-element.51.refs_3_, ...), custom_call_target="tpu_custom_call" | custom-call | flops 1 | bytes 1 | tf_op jit(solution)/shard_map/state/pallas_call | solution.py:200
  198.6 3.7 %collective-permute-start.49 = (bf16[2048,128]{1,0:T(8,128)(2,1)}, bf16[2048,128]{1,0:T(8,128)(2,1)S(1)}, u32[]{:S(2)}, u32[]{:S(2)}) collective-permute-start(bf16[2048,128]{1,0:T(8,128)(2,1)} %get-tuple-element.60), channel_id=1, source_target_pairs={{0,2},{2,0},{1,3},{3,1},{4,6},{6,4},{5,7},{7,5},{8,10},{10,8},{9,1... | collective-permute-start | bytes 1572872 | tf_op jit(solution)/shard_map/ppermute | solution.py:47
  202.3 1.7 collective-permute-done.49
  204.1 1.3 add_convert_fusion.1.refs_1_
  206.4 7.2 %state.3 = (f32[2048,128]{1,0:T(8,128)}, bf16[2048,128]{1,0:T(8,128)(2,1)}) custom-call(s32[18]{0:T(128)} %pad_add_fusion.4.info_ref, bf16[256,512]{1,0:T(8,128)(2,1)} %after.6.refs_0_, bf16[256,512]{1,0:T(8,128)(2,1)} %copy-done.16, bf16[256,512]{1,0:T(8,128)(2,1)} %copy-done.15, bf16[256,512]{1,0:T(8,128)(2,1)} %get-tuple-element.51.refs_3_, ...), custom_call_target="tpu_custom_call" | custom-call | flops 1 | bytes 1 | tf_op jit(solution)/shard_map/state/pallas_call | solution.py:200
  214.3 4.4 %collective-permute-done.51.refs_0_ = bf16[2048,128]{1,0:T(8,128)(2,1)S(1)} collective-permute-done((bf16[2048,128]{1,0:T(8,128)(2,1)S(1)}, bf16[2048,128]{1,0:T(8,128)(2,1)S(1)}, u32[]{:S(2)}, u32[]{:S(2)}) %collective-permute-start.51) | collective-permute-done | bytes 524320 | tf_op jit(solution)/shard_map/ppermute | solution.py:508
  220.4 3.5 %finish.1 = bf16[128,2048]{1,0:T(8,128)(2,1)} custom-call(bf16[2048,128]{1,0:T(8,128)(2,1)} %add_convert_fusion.own_ref, bf16[2048,128]{1,0:T(8,128)(2,1)} %after.7.got_ref), custom_call_target="tpu_custom_call" | custom-call | flops 524288 | bytes 1572864 | tf_op jit(solution)/shard_map/finish/pallas_call | solution.py:231
  (232 shorter events, 38.1 us)
Async XLA Ops:
  2.9 13.6 %collective-permute-start.4 = (bf16[256,1024]{1,0:T(8,128)(2,1)S(1)}, bf16[256,1024]{1,0:T(8,128)(2,1)S(1)}, u32[]{:S(2)}, u32[]{:S(2)}) collective-permute-start(bf16[256,1024]{1,0:T(8,128)(2,1)S(1)} %pad_maximum_fusion.2.refs_0_.refs_6_), channel_id=1, source_target_pairs={{0,8},{8,16},{16,24},{24,28},{28,20},{20,12},{12,4},{4,0},{1,9},{9... | collective-permute-start | bytes 1572872 | tf_op jit(solution)/shard_map/ppermute | solution.py:41
  4.4 13.1 %collective-permute-start.12 = (bf16[256,1024]{1,0:T(8,128)(2,1)S(1)}, bf16[256,1024]{1,0:T(8,128)(2,1)S(1)}, u32[]{:S(2)}, u32[]{:S(2)}) collective-permute-start(bf16[256,1024]{1,0:T(8,128)(2,1)S(1)} %collective-permute-done.7.refs_1_.refs_7_), channel_id=1, source_target_pairs={{8,0},{16,8},{24,16},{28,24},{20,28},{12,20},{4,12},{0,4},{9,1},{1... | collective-permute-start | bytes 1572872 | tf_op jit(solution)/shard_map/ppermute | solution.py:44
  5.7 23.2 %collective-permute-start.16 = (bf16[256,1024]{1,0:T(8,128)(2,1)S(1)}, bf16[256,1024]{1,0:T(8,128)(2,1)S(1)}, u32[]{:S(2)}, u32[]{:S(2)}) collective-permute-start(bf16[256,1024]{1,0:T(8,128)(2,1)S(1)} %pad_maximum_fusion.2.refs_0_.refs_6_), channel_id=1, source_target_pairs={{8,0},{16,8},{24,16},{28,24},{20,28},{12,20},{4,12},{0,4},{9,1},{1... | collective-permute-start | bytes 1572872 | tf_op jit(solution)/shard_map/ppermute | solution.py:44
  7.0 56.9 %collective-permute-start.3 = (bf16[128,4096]{1,0:T(8,128)(2,1)}, bf16[128,4096]{1,0:T(8,128)(2,1)}, u32[]{:S(2)}, u32[]{:S(2)}) collective-permute-start(bf16[128,4096]{1,0:T(8,128)(2,1)} %bitcast.7), channel_id=1, source_target_pairs={{0,2},{2,0},{1,3},{3,1},{4,6},{6,4},{5,7},{7,5},{8,10},{10,8},{9,1... | collective-permute-start | bytes 3145736 | tf_op jit(solution)/shard_map/ppermute | solution.py:47
  8.5 21.7 %collective-permute-start.8 = (bf16[256,1024]{1,0:T(8,128)(2,1)S(1)}, bf16[256,1024]{1,0:T(8,128)(2,1)S(1)}, u32[]{:S(2)}, u32[]{:S(2)}) collective-permute-start(bf16[256,1024]{1,0:T(8,128)(2,1)S(1)} %collective-permute-done.7.refs_1_.refs_7_), channel_id=1, source_target_pairs={{0,8},{8,16},{16,24},{24,28},{28,20},{20,12},{12,4},{4,0},{1,9},{9... | collective-permute-start | bytes 1572872 | tf_op jit(solution)/shard_map/ppermute | solution.py:41
  16.5 22.6 %collective-permute-start.5 = (bf16[256,1024]{1,0:T(8,128)(2,1)S(1)}, bf16[256,1024]{1,0:T(8,128)(2,1)}, u32[]{:S(2)}, u32[]{:S(2)}) collective-permute-start(bf16[256,1024]{1,0:T(8,128)(2,1)S(1)} %collective-permute-done.4.refs_2_.refs_8_), channel_id=1, source_target_pairs={{0,8},{8,16},{16,24},{24,28},{28,20},{20,12},{12,4},{4,0},{1,9},{9... | collective-permute-start | bytes 1572872 | tf_op jit(solution)/shard_map/ppermute | solution.py:41
  17.5 22.6 %collective-permute-start.13 = (bf16[256,1024]{1,0:T(8,128)(2,1)S(1)}, bf16[256,1024]{1,0:T(8,128)(2,1)}, u32[]{:S(2)}, u32[]{:S(2)}) collective-permute-start(bf16[256,1024]{1,0:T(8,128)(2,1)S(1)} %collective-permute-done.12.refs_9_.refs_21_), channel_id=1, source_target_pairs={{8,0},{16,8},{24,16},{28,24},{20,28},{12,20},{4,12},{0,4},{9,1},{1... | collective-permute-start | bytes 1572872 | tf_op jit(solution)/shard_map/ppermute | solution.py:44
  28.9 22.5 %collective-permute-start.17 = (bf16[256,1024]{1,0:T(8,128)(2,1)S(1)}, bf16[256,1024]{1,0:T(8,128)(2,1)}, u32[]{:S(2)}, u32[]{:S(2)}) collective-permute-start(bf16[256,1024]{1,0:T(8,128)(2,1)S(1)} %collective-permute-done.16.refs_8_.refs_20_), channel_id=1, source_target_pairs={{8,0},{16,8},{24,16},{28,24},{20,28},{12,20},{4,12},{0,4},{9,1},{1... | collective-permute-start | bytes 1572872 | tf_op jit(solution)/shard_map/ppermute | solution.py:44
  30.2 22.5 %collective-permute-start.9 = (bf16[256,1024]{1,0:T(8,128)(2,1)S(1)}, bf16[256,1024]{1,0:T(8,128)(2,1)}, u32[]{:S(2)}, u32[]{:S(2)}) collective-permute-start(bf16[256,1024]{1,0:T(8,128)(2,1)S(1)} %collective-permute-done.8.refs_3_.refs_9_), channel_id=1, source_target_pairs={{0,8},{8,16},{16,24},{24,28},{28,20},{20,12},{12,4},{4,0},{1,9},{9... | collective-permute-start | bytes 1572872 | tf_op jit(solution)/shard_map/ppermute | solution.py:41
  39.1 22.5 %collective-permute-start.6 = (bf16[256,1024]{1,0:T(8,128)(2,1)}, bf16[256,1024]{1,0:T(8,128)(2,1)}, u32[]{:S(2)}, u32[]{:S(2)}) collective-permute-start(bf16[256,1024]{1,0:T(8,128)(2,1)} %collective-permute-done.5.refs_4_.refs_10_), channel_id=1, source_target_pairs={{0,8},{8,16},{16,24},{24,28},{28,20},{20,12},{12,4},{4,0},{1,9},{9... | collective-permute-start | bytes 1572872 | tf_op jit(solution)/shard_map/ppermute | solution.py:41
  40.1 22.5 %collective-permute-start.14 = (bf16[256,1024]{1,0:T(8,128)(2,1)}, bf16[256,1024]{1,0:T(8,128)(2,1)}, u32[]{:S(2)}, u32[]{:S(2)}) collective-permute-start(bf16[256,1024]{1,0:T(8,128)(2,1)} %collective-permute-done.13.refs_7_.refs_19_), channel_id=1, source_target_pairs={{8,0},{16,8},{24,16},{28,24},{20,28},{12,20},{4,12},{0,4},{9,1},{1... | collective-permute-start | bytes 1572872 | tf_op jit(solution)/shard_map/ppermute | solution.py:44
  51.3 22.4 %collective-permute-start.18 = (bf16[256,1024]{1,0:T(8,128)(2,1)}, bf16[256,1024]{1,0:T(8,128)(2,1)S(1)}, u32[]{:S(2)}, u32[]{:S(2)}) collective-permute-start(bf16[256,1024]{1,0:T(8,128)(2,1)} %collective-permute-done.17.refs_6_.refs_18_), channel_id=1, source_target_pairs={{8,0},{16,8},{24,16},{28,24},{20,28},{12,20},{4,12},{0,4},{9,1},{1... | collective-permute-start | bytes 1572872 | tf_op jit(solution)/shard_map/ppermute | solution.py:44
  52.6 21.1 %collective-permute-start.10 = (bf16[256,1024]{1,0:T(8,128)(2,1)}, bf16[256,1024]{1,0:T(8,128)(2,1)S(1)}, u32[]{:S(2)}, u32[]{:S(2)}) collective-permute-start(bf16[256,1024]{1,0:T(8,128)(2,1)} %collective-permute-done.9.refs_5_.refs_11_), channel_id=1, source_target_pairs={{0,8},{8,16},{16,24},{24,28},{28,20},{20,12},{12,4},{4,0},{1,9},{9... | collective-permute-start | bytes 1572872 | tf_op jit(solution)/shard_map/ppermute | solution.py:41
  61.6 22.4 %collective-permute-start.11 = (bf16[256,1024]{1,0:T(8,128)(2,1)}, bf16[256,1024]{1,0:T(8,128)(2,1)S(1)}, u32[]{:S(2)}, u32[]{:S(2)}) collective-permute-start(bf16[256,1024]{1,0:T(8,128)(2,1)} %collective-permute-done.6.refs_0_.refs_12_), channel_id=1, source_target_pairs={{0,8},{8,16},{16,24},{24,28},{28,20},{20,12},{12,4},{4,0},{1,9},{9... | collective-permute-start | bytes 1572872 | tf_op jit(solution)/shard_map/ppermute | solution.py:41
  62.6 22.4 %collective-permute-start.15 = (bf16[256,1024]{1,0:T(8,128)(2,1)}, bf16[256,1024]{1,0:T(8,128)(2,1)S(1)}, u32[]{:S(2)}, u32[]{:S(2)}) collective-permute-start(bf16[256,1024]{1,0:T(8,128)(2,1)} %collective-permute-done.14.refs_5_.refs_17_), channel_id=1, source_target_pairs={{8,0},{16,8},{24,16},{28,24},{20,28},{12,20},{4,12},{0,4},{9,1},{1... | collective-permute-start | bytes 1572872 | tf_op jit(solution)/shard_map/ppermute | solution.py:44
  87.8 6.7 %collective-permute-start.19 = (bf16[256,512]{1,0:T(8,128)(2,1)S(1)}, bf16[256,512]{1,0:T(8,128)(2,1)S(1)}, u32[]{:S(2)}, u32[]{:S(2)}) collective-permute-start(bf16[256,512]{1,0:T(8,128)(2,1)S(1)} %get-tuple-element.33.refs_4_), channel_id=1, source_target_pairs={{0,8},{8,16},{16,24},{24,28},{28,20},{20,12},{12,4},{4,0},{1,9},{9... | collective-permute-start | bytes 786440 | tf_op jit(solution)/shard_map/ppermute | solution.py:41
  88.1 9.4 %collective-permute-start.23 = (bf16[256,512]{1,0:T(8,128)(2,1)S(1)}, bf16[256,512]{1,0:T(8,128)(2,1)S(1)}, u32[]{:S(2)}, u32[]{:S(2)}) collective-permute-start(bf16[256,512]{1,0:T(8,128)(2,1)S(1)} %get-tuple-element.33.refs_4_), channel_id=1, source_target_pairs={{8,0},{16,8},{24,16},{28,24},{20,28},{12,20},{4,12},{0,4},{9,1},{1... | collective-permute-start | bytes 786440 | tf_op jit(solution)/shard_map/ppermute | solution.py:44
  89.4 9.5 %collective-permute-start = (s32[8,3]{0,1:T(4,128)S(1)}, s32[8,3]{0,1:T(4,128)S(1)}, u32[]{:S(2)}, u32[]{:S(2)}) collective-permute-start(s32[8,3]{0,1:T(4,128)S(1)} %get-tuple-element.77), channel_id=1, source_target_pairs={{0,2},{2,0},{1,3},{3,1},{4,6},{6,4},{5,7},{7,5},{8,10},{10,8},{9,1... | collective-permute-start | bytes 296 | tf_op jit(solution)/shard_map/ppermute | solution.py:47
  94.7 13.3 %collective-permute-start.1 = (bf16[512,512]{1,0:T(8,128)(2,1)S(1)}, bf16[512,512]{1,0:T(8,128)(2,1)S(1)}, u32[]{:S(2)}, u32[]{:S(2)}) collective-permute-start(bf16[512,512]{1,0:T(8,128)(2,1)S(1)} %constant_dynamic-slice_fusion.9), channel_id=1, source_target_pairs={{0,2},{2,0},{1,3},{3,1},{4,6},{6,4},{5,7},{7,5},{8,10},{10,8},{9,1... | collective-permute-start | bytes 1572872 | tf_op jit(solution)/shard_map/ppermute | solution.py:47
  97.2 17.8 %collective-permute-start.2 = (bf16[512,512]{1,0:T(8,128)(2,1)S(1)}, bf16[512,512]{1,0:T(8,128)(2,1)S(1)}, u32[]{:S(2)}, u32[]{:S(2)}) collective-permute-start(bf16[512,512]{1,0:T(8,128)(2,1)S(1)} %constant_dynamic-slice_fusion.8), channel_id=1, source_target_pairs={{0,2},{2,0},{1,3},{3,1},{4,6},{6,4},{5,7},{7,5},{8,10},{10,8},{9,1... | collective-permute-start | bytes 1572872 | tf_op jit(solution)/shard_map/ppermute | solution.py:47
  97.5 7.5 %collective-permute-start.24 = (bf16[256,512]{1,0:T(8,128)(2,1)S(1)}, bf16[256,512]{1,0:T(8,128)(2,1)S(1)}, u32[]{:S(2)}, u32[]{:S(2)}) collective-permute-start(bf16[256,512]{1,0:T(8,128)(2,1)S(1)} %collective-permute-done.23.refs_11_), channel_id=1, source_target_pairs={{8,0},{16,8},{24,16},{28,24},{20,28},{12,20},{4,12},{0,4},{9,1},{1... | collective-permute-start | bytes 786440 | tf_op jit(solution)/shard_map/ppermute | solution.py:44
  100.2 9.1 %collective-permute-start.21 = (bf16[256,512]{1,0:T(8,128)(2,1)S(1)}, bf16[256,512]{1,0:T(8,128)(2,1)}, u32[]{:S(2)}, u32[]{:S(2)}) collective-permute-start(bf16[256,512]{1,0:T(8,128)(2,1)S(1)} %collective-permute-done.20.refs_6_.refs_1_), channel_id=1, source_target_pairs={{0,8},{8,16},{16,24},{24,28},{28,20},{20,12},{12,4},{4,0},{1,9},{9... | collective-permute-start | bytes 786440 | tf_op jit(solution)/shard_map/ppermute | solution.py:41
  105.7 6.7 %collective-permute-start.29 = (bf16[256,512]{1,0:T(8,128)(2,1)}, bf16[256,512]{1,0:T(8,128)(2,1)S(1)}, u32[]{:S(2)}, u32[]{:S(2)}) collective-permute-start(bf16[256,512]{1,0:T(8,128)(2,1)} %after.4.refs_4_), channel_id=1, source_target_pairs={{8,0},{16,8},{24,16},{28,24},{20,28},{12,20},{4,12},{0,4},{9,1},{1... | collective-permute-start | bytes 786440 | tf_op jit(solution)/shard_map/ppermute | solution.py:44
  107.8 7.1 %collective-permute-start.26 = (bf16[256,512]{1,0:T(8,128)(2,1)}, bf16[256,512]{1,0:T(8,128)(2,1)}, u32[]{:S(2)}, u32[]{:S(2)}) collective-permute-start(bf16[256,512]{1,0:T(8,128)(2,1)} %after.4.refs_4_), channel_id=1, source_target_pairs={{0,8},{8,16},{16,24},{24,28},{28,20},{20,12},{12,4},{4,0},{1,9},{9... | collective-permute-start | bytes 786440 | tf_op jit(solution)/shard_map/ppermute | solution.py:41
  108.0 10.1 %collective-permute-start.25 = (bf16[256,512]{1,0:T(8,128)(2,1)}, bf16[256,512]{1,0:T(8,128)(2,1)S(1)}, u32[]{:S(2)}, u32[]{:S(2)}) collective-permute-start(bf16[256,512]{1,0:T(8,128)(2,1)} %copy-done.38), channel_id=1, source_target_pairs={{8,0},{16,8},{24,16},{28,24},{20,28},{12,20},{4,12},{0,4},{9,1},{1... | collective-permute-start | bytes 786440 | tf_op jit(solution)/shard_map/ppermute | solution.py:44
  109.3 10.5 %collective-permute-start.22 = (bf16[256,512]{1,0:T(8,128)(2,1)}, bf16[256,512]{1,0:T(8,128)(2,1)S(1)}, u32[]{:S(2)}, u32[]{:S(2)}) collective-permute-start(bf16[256,512]{1,0:T(8,128)(2,1)} %collective-permute-done.21.refs_7_), channel_id=1, source_target_pairs={{0,8},{8,16},{16,24},{24,28},{28,20},{20,12},{12,4},{4,0},{1,9},{9... | collective-permute-start | bytes 786440 | tf_op jit(solution)/shard_map/ppermute | solution.py:41
  112.4 19.9 %collective-permute-start.30 = (bf16[256,512]{1,0:T(8,128)(2,1)S(1)}, bf16[256,512]{1,0:T(8,128)(2,1)S(1)}, u32[]{:S(2)}, u32[]{:S(2)}) collective-permute-start(bf16[256,512]{1,0:T(8,128)(2,1)S(1)} %collective-permute-done.29.refs_11_), channel_id=1, source_target_pairs={{8,0},{16,8},{24,16},{28,24},{20,28},{12,20},{4,12},{0,4},{9,1},{1... | collective-permute-start | bytes 786440 | tf_op jit(solution)/shard_map/ppermute | solution.py:44
  114.9 21.4 %collective-permute-start.27 = (bf16[256,512]{1,0:T(8,128)(2,1)}, bf16[256,512]{1,0:T(8,128)(2,1)}, u32[]{:S(2)}, u32[]{:S(2)}) collective-permute-start(bf16[256,512]{1,0:T(8,128)(2,1)} %collective-permute-done.26.refs_5_), channel_id=1, source_target_pairs={{0,8},{8,16},{16,24},{24,28},{28,20},{20,12},{12,4},{4,0},{1,9},{9... | collective-permute-start | bytes 786440 | tf_op jit(solution)/shard_map/ppermute | solution.py:41
  131.0 10.3 %collective-permute-start.39 = (bf16[256,512]{1,0:T(8,128)(2,1)}, bf16[256,512]{1,0:T(8,128)(2,1)S(1)}, u32[]{:S(2)}, u32[]{:S(2)}) collective-permute-start(bf16[256,512]{1,0:T(8,128)(2,1)} %get-tuple-element.50), channel_id=1, source_target_pairs={{8,0},{16,8},{24,16},{28,24},{20,28},{12,20},{4,12},{0,4},{9,1},{1... | collective-permute-start | bytes 786440 | tf_op jit(solution)/shard_map/ppermute | solution.py:44
  132.3 7.6 %collective-permute-start.31 = (bf16[256,512]{1,0:T(8,128)(2,1)S(1)}, bf16[256,512]{1,0:T(8,128)(2,1)S(1)}, u32[]{:S(2)}, u32[]{:S(2)}) collective-permute-start(bf16[256,512]{1,0:T(8,128)(2,1)S(1)} %collective-permute-done.30.refs_10_), channel_id=1, source_target_pairs={{8,0},{16,8},{24,16},{28,24},{20,28},{12,20},{4,12},{0,4},{9,1},{1... | collective-permute-start | bytes 786440 | tf_op jit(solution)/shard_map/ppermute | solution.py:44
  134.2 8.4 %collective-permute-start.35 = (bf16[256,512]{1,0:T(8,128)(2,1)}, bf16[256,512]{1,0:T(8,128)(2,1)S(1)}, u32[]{:S(2)}, u32[]{:S(2)}) collective-permute-start(bf16[256,512]{1,0:T(8,128)(2,1)} %get-tuple-element.47), channel_id=1, source_target_pairs={{0,8},{8,16},{16,24},{24,28},{28,20},{20,12},{12,4},{4,0},{1,9},{9... | collective-permute-start | bytes 786440 | tf_op jit(solution)/shard_map/ppermute | solution.py:41
  136.3 6.6 %collective-permute-start.28 = (bf16[256,512]{1,0:T(8,128)(2,1)}, bf16[256,512]{1,0:T(8,128)(2,1)S(1)}, u32[]{:S(2)}, u32[]{:S(2)}) collective-permute-start(bf16[256,512]{1,0:T(8,128)(2,1)} %collective-permute-done.27.refs_6_), channel_id=1, source_target_pairs={{0,8},{8,16},{16,24},{24,28},{28,20},{20,12},{12,4},{4,0},{1,9},{9... | collective-permute-start | bytes 786440 | tf_op jit(solution)/shard_map/ppermute | solution.py:41
  139.9 8.1 %collective-permute-start.32 = (bf16[256,512]{1,0:T(8,128)(2,1)S(1)}, bf16[256,512]{1,0:T(8,128)(2,1)S(1)}, u32[]{:S(2)}, u32[]{:S(2)}) collective-permute-start(bf16[256,512]{1,0:T(8,128)(2,1)S(1)} %collective-permute-done.31.refs_9_), channel_id=1, source_target_pairs={{8,0},{16,8},{24,16},{28,24},{20,28},{12,20},{4,12},{0,4},{9,1},{1... | collective-permute-start | bytes 786440 | tf_op jit(solution)/shard_map/ppermute | solution.py:44
  141.3 19.4 %collective-permute-start.40 = (bf16[256,512]{1,0:T(8,128)(2,1)S(1)}, bf16[256,512]{1,0:T(8,128)(2,1)S(1)}, u32[]{:S(2)}, u32[]{:S(2)}) collective-permute-start(bf16[256,512]{1,0:T(8,128)(2,1)S(1)} %add_convert_fusion.8), channel_id=1, source_target_pairs={{8,0},{16,8},{24,16},{28,24},{20,28},{12,20},{4,12},{0,4},{9,1},{1... | collective-permute-start | bytes 786440 | tf_op jit(solution)/shard_map/ppermute | solution.py:44
  142.7 19.6 %collective-permute-start.36 = (bf16[256,512]{1,0:T(8,128)(2,1)S(1)}, bf16[256,512]{1,0:T(8,128)(2,1)S(1)}, u32[]{:S(2)}, u32[]{:S(2)}) collective-permute-start(bf16[256,512]{1,0:T(8,128)(2,1)S(1)} %add_convert_fusion.11), channel_id=1, source_target_pairs={{0,8},{8,16},{16,24},{24,28},{28,20},{20,12},{12,4},{4,0},{1,9},{9... | collective-permute-start | bytes 786440 | tf_op jit(solution)/shard_map/ppermute | solution.py:41
  159.2 11.3 %collective-permute-start.45 = (bf16[256,512]{1,0:T(8,128)(2,1)}, bf16[256,512]{1,0:T(8,128)(2,1)S(1)}, u32[]{:S(2)}, u32[]{:S(2)}) collective-permute-start(bf16[256,512]{1,0:T(8,128)(2,1)} %get-tuple-element.58), channel_id=1, source_target_pairs={{8,0},{16,8},{24,16},{28,24},{20,28},{12,20},{4,12},{0,4},{9,1},{1... | collective-permute-start | bytes 786440 | tf_op jit(solution)/shard_map/ppermute | solution.py:44
  160.5 11.8 %collective-permute-start.42 = (bf16[256,512]{1,0:T(8,128)(2,1)}, bf16[256,512]{1,0:T(8,128)(2,1)S(1)}, u32[]{:S(2)}, u32[]{:S(2)}) collective-permute-start(bf16[256,512]{1,0:T(8,128)(2,1)} %get-tuple-element.54), channel_id=1, source_target_pairs={{0,8},{8,16},{16,24},{24,28},{28,20},{20,12},{12,4},{4,0},{1,9},{9... | collective-permute-start | bytes 786440 | tf_op jit(solution)/shard_map/ppermute | solution.py:41
  160.8 28.5 %collective-permute-start.41 = (bf16[256,512]{1,0:T(8,128)(2,1)S(1)}, bf16[256,512]{1,0:T(8,128)(2,1)S(1)}, u32[]{:S(2)}, u32[]{:S(2)}) collective-permute-start(bf16[256,512]{1,0:T(8,128)(2,1)S(1)} %add_convert_fusion.7), channel_id=1, source_target_pairs={{8,0},{16,8},{24,16},{28,24},{20,28},{12,20},{4,12},{0,4},{9,1},{1... | collective-permute-start | bytes 786440 | tf_op jit(solution)/shard_map/ppermute | solution.py:44
  162.4 11.3 %collective-permute-start.37 = (bf16[256,512]{1,0:T(8,128)(2,1)S(1)}, bf16[256,512]{1,0:T(8,128)(2,1)S(1)}, u32[]{:S(2)}, u32[]{:S(2)}) collective-permute-start(bf16[256,512]{1,0:T(8,128)(2,1)S(1)} %add_convert_fusion.10), channel_id=1, source_target_pairs={{0,8},{8,16},{16,24},{24,28},{28,20},{20,12},{12,4},{4,0},{1,9},{9... | collective-permute-start | bytes 786440 | tf_op jit(solution)/shard_map/ppermute | solution.py:41
  162.7 11.4 %collective-permute-start.34 = (bf16[512,512]{1,0:T(8,128)(2,1)S(1)}, bf16[512,512]{1,0:T(8,128)(2,1)S(1)}, u32[]{:S(2)}, u32[]{:S(2)}) collective-permute-start(bf16[512,512]{1,0:T(8,128)(2,1)S(1)} %pad_maximum_fusion.5), channel_id=1, source_target_pairs={{0,2},{2,0},{1,3},{3,1},{4,6},{6,4},{5,7},{7,5},{8,10},{10,8},{9,1... | collective-permute-start | bytes 1572872 | tf_op jit(solution)/shard_map/ppermute | solution.py:47
  170.4 10.0 %collective-permute-start.33 = (bf16[512,512]{1,0:T(8,128)(2,1)S(1)}, bf16[512,512]{1,0:T(8,128)(2,1)S(1)}, u32[]{:S(2)}, u32[]{:S(2)}) collective-permute-start(bf16[512,512]{1,0:T(8,128)(2,1)S(1)} %pad_maximum_fusion.4), channel_id=1, source_target_pairs={{0,2},{2,0},{1,3},{3,1},{4,6},{6,4},{5,7},{7,5},{8,10},{10,8},{9,1... | collective-permute-start | bytes 1572872 | tf_op jit(solution)/shard_map/ppermute | solution.py:47
  172.3 6.4 %collective-permute-start.46 = (bf16[256,512]{1,0:T(8,128)(2,1)S(1)}, bf16[256,512]{1,0:T(8,128)(2,1)S(1)}, u32[]{:S(2)}, u32[]{:S(2)}) collective-permute-start(bf16[256,512]{1,0:T(8,128)(2,1)S(1)} %add_convert_fusion.4), channel_id=1, source_target_pairs={{8,0},{16,8},{24,16},{28,24},{20,28},{12,20},{4,12},{0,4},{9,1},{1... | collective-permute-start | bytes 786440 | tf_op jit(solution)/shard_map/ppermute | solution.py:44
  173.7 6.7 %collective-permute-start.43 = (bf16[256,512]{1,0:T(8,128)(2,1)S(1)}, bf16[256,512]{1,0:T(8,128)(2,1)S(1)}, u32[]{:S(2)}, u32[]{:S(2)}) collective-permute-start(bf16[256,512]{1,0:T(8,128)(2,1)S(1)} %add_convert_fusion.6), channel_id=1, source_target_pairs={{0,8},{8,16},{16,24},{24,28},{28,20},{20,12},{12,4},{4,0},{1,9},{9... | collective-permute-start | bytes 786440 | tf_op jit(solution)/shard_map/ppermute | solution.py:41
  174.1 15.3 %collective-permute-start.38 = (bf16[256,512]{1,0:T(8,128)(2,1)S(1)}, bf16[256,512]{1,0:T(8,128)(2,1)S(1)}, u32[]{:S(2)}, u32[]{:S(2)}) collective-permute-start(bf16[256,512]{1,0:T(8,128)(2,1)S(1)} %add_convert_fusion.9), channel_id=1, source_target_pairs={{0,8},{8,16},{16,24},{24,28},{28,20},{20,12},{12,4},{4,0},{1,9},{9... | collective-permute-start | bytes 786440 | tf_op jit(solution)/shard_map/ppermute | solution.py:41
  180.6 9.5 %collective-permute-start.44 = (bf16[256,512]{1,0:T(8,128)(2,1)S(1)}, bf16[256,512]{1,0:T(8,128)(2,1)S(1)}, u32[]{:S(2)}, u32[]{:S(2)}) collective-permute-start(bf16[256,512]{1,0:T(8,128)(2,1)S(1)} %add_convert_fusion.5), channel_id=1, source_target_pairs={{0,8},{8,16},{16,24},{24,28},{28,20},{20,12},{12,4},{4,0},{1,9},{9... | collective-permute-start | bytes 786440 | tf_op jit(solution)/shard_map/ppermute | solution.py:41
  184.4 6.0 %collective-permute-start.48 = (bf16[256,512]{1,0:T(8,128)(2,1)S(1)}, bf16[256,512]{1,0:T(8,128)(2,1)S(1)}, u32[]{:S(2)}, u32[]{:S(2)}) collective-permute-start(bf16[256,512]{1,0:T(8,128)(2,1)S(1)} %add_convert_fusion.2), channel_id=1, source_target_pairs={{8,0},{16,8},{24,16},{28,24},{20,28},{12,20},{4,12},{0,4},{9,1},{1... | collective-permute-start | bytes 786440 | tf_op jit(solution)/shard_map/ppermute | solution.py:44
  205.4 13.2 %collective-permute-start.51 = (bf16[2048,128]{1,0:T(8,128)(2,1)S(1)}, bf16[2048,128]{1,0:T(8,128)(2,1)S(1)}, u32[]{:S(2)}, u32[]{:S(2)}) collective-permute-start(bf16[2048,128]{1,0:T(8,128)(2,1)S(1)} %add_convert_fusion.1.refs_1_), channel_id=1, source_target_pairs={{0,1},{1,0},{2,3},{3,2},{4,5},{5,4},{6,7},{7,6},{8,9},{9,8},{10,11... | collective-permute-start | bytes 1572872 | tf_op jit(solution)/shard_map/ppermute | solution.py:508
  213.6 5.9 %collective-permute-start.50 = (bf16[2048,128]{1,0:T(8,128)(2,1)}, bf16[2048,128]{1,0:T(8,128)(2,1)S(1)}, u32[]{:S(2)}, u32[]{:S(2)}) collective-permute-start(bf16[2048,128]{1,0:T(8,128)(2,1)} %get-tuple-element.62), channel_id=1, source_target_pairs={{0,2},{2,0},{1,3},{3,1},{4,6},{6,4},{5,7},{7,5},{8,10},{10,8},{9,1... | collective-permute-start | bytes 1572872 | tf_op jit(solution)/shard_map/ppermute | solution.py:47
  (58 other events, 687.6 us)

commit v2 on v1

--- a/solution.py
+++ b/solution.py
@@ -163,8 +163,11 @@
 
 def state_kernel(chunks, count, depth, dmodel, offset, info_ref, *refs):
     sums, weights, refs = refs[: 3 * chunks], refs[3 * chunks : 3 * chunks + count], refs[3 * chunks + count :]
-    out_mine, out_pair, right, held, sems = refs
+    out_mine, out_pair, right, held, terms, sems, term_sems = refs
     tokens = right.shape[1] // 2
+    copies = [pltpu.make_async_copy(x, terms.at[i], term_sems.at[i]) for i, x in enumerate(sums)]
+    for copy in copies:
+        copy.start()
     features = held.shape[0]
     part = features // PARTS
     for p, view in enumerate(pieces(weights, depth)):
@@ -178,7 +181,9 @@
 
     width = sums[0].shape[1]
     for k in range(chunks):
-        own, up, down = (sums[3 * k + j][...].astype(F32) for j in range(3))
+        for copy in copies[3 * k : 3 * k + 3]:
+            copy.wait()
+        own, up, down = (terms[3 * k + j].astype(F32) for j in range(3))
         right[k * width : (k + 1) * width, :] = (own + up + down).astype(BF16).T
     second = info_ref[1] == 1
     for b in range(PARTS):
@@ -204,13 +209,14 @@
             jax.ShapeDtypeStruct((features, tokens // 2), BF16),
         ],
         in_specs=[pl.BlockSpec(memory_space=pltpu.SMEM)]
-        + [vmem] * len(flat_sums)
-        + [hbm] * len(flat),
+        + [hbm] * (len(flat_sums) + len(flat)),
         out_specs=[vmem, vmem],
         scratch_shapes=[
             pltpu.VMEM((width, tokens), BF16),
             pltpu.VMEM((features, width), BF16),
+            pltpu.VMEM((len(flat_sums),) + flat_sums[0].shape, BF16),
             pltpu.SemaphoreType.DMA((PARTS,)),
+            pltpu.SemaphoreType.DMA((len(flat_sums),)),
         ],
         compiler_params=pltpu.CompilerParams(
             vmem_limit_bytes=60 * 1024 * 1024
@@ -220,26 +226,24 @@
     )(info, *flat_sums, *flat)
 
 
-def final_kernel(own_ref, got_ref, out_ref):
-    out_ref[...] = (own_ref[...].astype(F32) + got_ref[...].astype(F32)).T.astype(BF16)
-
-
-def finish(own, got):
-    features, tokens = own.shape
-    block = features // PARTS
-    part = pl.BlockSpec((block, tokens), lambda i: (i, 0))
+def final_kernel(mine_ref, came_ref, got_ref, out_ref):
+    term = (mine_ref[...] + came_ref[...].astype(F32)).astype(BF16)
+    out_ref[...] = (term.astype(F32) + got_ref[...].astype(F32)).T.astype(BF16)
+
+
+def finish(mine, came, got):
+    vmem = pl.BlockSpec(memory_space=pltpu.VMEM)
     return pl.pallas_call(
         final_kernel,
-        out_shape=jax.ShapeDtypeStruct((tokens, features), BF16),
-        grid=(PARTS,),
-        in_specs=[part, part],
-        out_specs=pl.BlockSpec((tokens, block), lambda i: (0, i)),
-        compiler_params=pltpu.CompilerParams(vmem_limit_bytes=60 * 1024 * 1024),
+        out_shape=jax.ShapeDtypeStruct(mine.shape[::-1], BF16),
+        in_specs=[vmem, vmem, vmem],
+        out_specs=vmem,
+        compiler_params=pltpu.CompilerParams(vmem_limit_bytes=room((mine.shape, 28))),
         cost_estimate=pl.CostEstimate(
-            flops=2 * own.size, bytes_accessed=6 * own.size, transcendentals=0
+            flops=2 * mine.size, bytes_accessed=10 * mine.size, transcendentals=0
         ),
         name="finish",
-    )(own, got)
+    )(mine, came, got)
 
 
 def attend_kernel(blocks, heads, spans, neigh, offset, slot_ref, count_ref, *refs):
@@ -291,9 +295,10 @@
                     jnp.concatenate([right[h, j] for j in range(neigh)], axis=axis),
                     preferred_element_type=F32,
                 )
+                columns = both.shape[1] // neigh
                 for j in range(neigh):
                     at = slice(j * span_len, (j + 1) * span_len)
-                    out[h, j] = both[at, j * HEAD : (j + 1) * HEAD]
+                    out[h, j] = both[at, j * columns : (j + 1) * columns]
             return out
 
         length = rows.shape[1]
@@ -503,11 +508,12 @@
         term_mine, term_pair = state_terms(
             info, (s - 1) * wide, wide, depth, dmodel, ends, weights
         )
-        term = (term_mine + ring.other(term_pair).astype(F32)).astype(BF16)
+        came = ring.other(term_pair)
         if s < tensors:
+            term = (term_mine + came.astype(F32)).astype(BF16)
             went = lax.ppermute(term, "tensor", [(i, (i + s) % tensors) for i in range(tensors)])
             got = went if got is None else got.astype(F32) + went.astype(F32)
-    final = finish(term, after(got, cost=20_000_000_000))
+    final = finish(term_mine, came, after(got, cost=20_000_000_000))
     return swap_out[0], swap_out[1], final.reshape((1,) + final.shape)
 
 

time: 228 us -> 225 us (0.987)
  Pallas kernels: 45.5 us -> 43 us
    pallas_call x1, Pallas kernels: 3.49 us -> 1.09 us  [finish(): pl.pallas_call(final_kernel, out_shape=jax.ShapeDtypeStruct(mine.shape[::...]
    unnamed x110 -> x112, local copies, waits for them, and re-layouts: 5.78 us -> 6.82 us
where the time goes in v2:
time: 225 us; the launch traced here: 222 us
  waiting for transfers between devices  102 us (45%)
  starting transfers between devices  54.1 us (24%)
  Pallas kernels  43 us (19%)
  local copies, waits for them, and re-layouts  11.9 us (5%)
  other arithmetic  8.87 us (4%)
    ppermute x21, waiting for transfers between devices, ccw(): return lax.ppermute(x, 'chip', self.down)  52.5 us
    ppermute x21, waiting for transfers between devices, cw(): return lax.ppermute(x, 'chip', self.up)  42.4 us
    ppermute x21, starting transfers between devices, ccw(): return lax.ppermute(x, 'chip', self.down)  29.3 us
    pallas_call x2, Pallas kernels, attend(): pl.pallas_call(functools.partial(attend_kernel, blocks, heads, spans, nei...  20.8 us
    ppermute x9, starting transfers between devices, other(): return lax.ppermute(x, 'core', [(0, 1), (1, 0)])  20 us
    pallas_call x2, Pallas kernels, state_terms(): pl.pallas_call(functools.partial(state_kernel, len(sums), len(flat), dept...  14.6 us
    unnamed x112, local copies, waits for them, and re-layouts  6.82 us
    pallas_call x2, Pallas kernels, add_rows(): pl.pallas_call(functools.partial(rows_kernel, len(flat), depth, before is...  6.63 us
  transfers between devices with their start and end apart: 52, of which 26 were waited for; matrix products, arithmetic and copies ran while one was open for 6% of the time, Pallas kernels for 14%

profile of v2, /device:TPU:13, one launch (start us, length us, event | category | flops | bytes accessed | tf_op | source)
XLA Modules:
  0.0 221.5 jit_solution(644171126480674200)
XLA Ops:
  0.6 1.4 constant_dynamic-slice_fusion.2
  8.7 7.8 %collective-permute-done.4.refs_2_.refs_8_ = bf16[256,1024]{1,0:T(8,128)(2,1)S(1)} collective-permute-done((bf16[256,1024]{1,0:T(8,128)(2,1)S(1)}, bf16[256,1024]{1,0:T(8,128)(2,1)S(1)}, u32[]{:S(2)}, u32[]{:S(2)}) %collective-permute-start.4) | collective-permute-done | bytes 524320 | tf_op jit(solution)/shard_map/ppermute | solution.py:41
  20.2 8.7 %collective-permute-done.16.refs_8_.refs_20_ = bf16[256,1024]{1,0:T(8,128)(2,1)S(1)} collective-permute-done((bf16[256,1024]{1,0:T(8,128)(2,1)S(1)}, bf16[256,1024]{1,0:T(8,128)(2,1)S(1)}, u32[]{:S(2)}, u32[]{:S(2)}) %collective-permute-start.16) | collective-permute-done | bytes 524320 | tf_op jit(solution)/shard_map/ppermute | solution.py:44
  28.9 1.3 collective-permute-start.17
  30.3 8.7 %collective-permute-done.5.refs_4_.refs_10_ = bf16[256,1024]{1,0:T(8,128)(2,1)} collective-permute-done((bf16[256,1024]{1,0:T(8,128)(2,1)S(1)}, bf16[256,1024]{1,0:T(8,128)(2,1)}, u32[]{:S(2)}, u32[]{:S(2)}) %collective-permute-start.5) | collective-permute-done | bytes 524320 | tf_op jit(solution)/shard_map/ppermute | solution.py:41
  40.1 1.3 collective-permute-start.14
  42.0 9.3 %collective-permute-done.17.refs_6_.refs_18_ = bf16[256,1024]{1,0:T(8,128)(2,1)} collective-permute-done((bf16[256,1024]{1,0:T(8,128)(2,1)S(1)}, bf16[256,1024]{1,0:T(8,128)(2,1)}, u32[]{:S(2)}, u32[]{:S(2)}) %collective-permute-start.17) | collective-permute-done | bytes 524320 | tf_op jit(solution)/shard_map/ppermute | solution.py:44
  51.3 1.3 collective-permute-start.18
  52.8 8.8 %collective-permute-done.6.refs_0_.refs_12_ = bf16[256,1024]{1,0:T(8,128)(2,1)} collective-permute-done((bf16[256,1024]{1,0:T(8,128)(2,1)}, bf16[256,1024]{1,0:T(8,128)(2,1)}, u32[]{:S(2)}, u32[]{:S(2)}) %collective-permute-start.6) | collective-permute-done | bytes 524320 | tf_op jit(solution)/shard_map/ppermute | solution.py:41
  62.6 1.3 collective-permute-start.15
  63.9 1.7 broadcast_select_fusion
  65.6 3.8 %rows.2.refs_6_ = f32[256,1024]{1,0:T(8,128)S(1)} custom-call(s32[10]{0:T(128)S(1)} %reshape.169.feature_ref, bf16[128,4096]{1,0:T(8,128)(2,1)S(1)} %get-tuple-element.64.low_ref, bf16[128,4096]{1,0:T(8,128)(2,1)S(1)} %get-tuple-element.63.high_ref, bf16[256,1024]{1,0:T(8,128)(2,1)S(1)} %pad_maximum_fusion.2.refs_0_.refs_6_, ...), custom_call_target="tpu_custom_call" | custom-call | flops 4026531840 | bytes 5242880 | tf_op jit(solution)/shard_map/rows/pallas_call | solution.py:137
  69.5 4.2 %collective-permute-done.18.refs_4_.refs_16_ = bf16[256,1024]{1,0:T(8,128)(2,1)S(1)} collective-permute-done((bf16[256,1024]{1,0:T(8,128)(2,1)}, bf16[256,1024]{1,0:T(8,128)(2,1)S(1)}, u32[]{:S(2)}, u32[]{:S(2)}) %collective-permute-start.18) | collective-permute-done | bytes 524320 | tf_op jit(solution)/shard_map/ppermute | solution.py:44
  73.7 10.2 %collective-permute-done.11.refs_2_.refs_14_ = bf16[256,1024]{1,0:T(8,128)(2,1)S(1)} collective-permute-done((bf16[256,1024]{1,0:T(8,128)(2,1)}, bf16[256,1024]{1,0:T(8,128)(2,1)S(1)}, u32[]{:S(2)}, u32[]{:S(2)}) %collective-permute-start.11) | collective-permute-done | bytes 524320 | tf_op jit(solution)/shard_map/ppermute | solution.py:41
  84.9 2.8 %rows.3 = (bf16[256,512]{1,0:T(8,128)(2,1)S(1)}, bf16[256,512]{1,0:T(8,128)(2,1)S(1)}) custom-call(s32[6]{0:T(128)S(1)} %reshape.167.feature_ref, bf16[128,4096]{1,0:T(8,128)(2,1)S(1)} %get-tuple-element.64.low_ref, bf16[128,4096]{1,0:T(8,128)(2,1)S(1)} %get-tuple-element.63.high_ref, bf16[256,1024]{1,0:T(8,128)(2,1)} %collective-permute-done.6.refs_0_.refs_12_, ...), custom_call_target="tpu_custom_call" | custom-call | flops 2415919104 | bytes 3145728 | tf_op jit(solution)/shard_map/rows/pallas_call | solution.py:137
  89.4 1.8 collective-permute-start
  91.2 3.3 %collective-permute-done.19.refs_5_ = bf16[256,512]{1,0:T(8,128)(2,1)S(1)} collective-permute-done((bf16[256,512]{1,0:T(8,128)(2,1)S(1)}, bf16[256,512]{1,0:T(8,128)(2,1)S(1)}, u32[]{:S(2)}, u32[]{:S(2)}) %collective-permute-start.19) | collective-permute-done | bytes 262176 | tf_op jit(solution)/shard_map/ppermute | solution.py:41
  94.7 2.5 %collective-permute-start.1 = (bf16[512,512]{1,0:T(8,128)(2,1)S(1)}, bf16[512,512]{1,0:T(8,128)(2,1)S(1)}, u32[]{:S(2)}, u32[]{:S(2)}) collective-permute-start(bf16[512,512]{1,0:T(8,128)(2,1)S(1)} %constant_dynamic-slice_fusion.9), channel_id=1, source_target_pairs={{0,2},{2,0},{1,3},{3,1},{4,6},{6,4},{5,7},{7,5},{8,10},{10,8},{9,1... | collective-permute-start | bytes 1572872 | tf_op jit(solution)/shard_map/ppermute | solution.py:47
  97.5 1.3 collective-permute-start.24
  100.4 4.6 %collective-permute-done.24.refs_10_.refs_2_ = bf16[256,512]{1,0:T(8,128)(2,1)S(1)} collective-permute-done((bf16[256,512]{1,0:T(8,128)(2,1)S(1)}, bf16[256,512]{1,0:T(8,128)(2,1)S(1)}, u32[]{:S(2)}, u32[]{:S(2)}) %collective-permute-start.24) | collective-permute-done | bytes 262176 | tf_op jit(solution)/shard_map/ppermute | solution.py:44
  105.7 1.3 collective-permute-start.29
  108.0 1.3 collective-permute-start.25
  110.1 2.3 %collective-permute-done.29.refs_11_ = bf16[256,512]{1,0:T(8,128)(2,1)S(1)} collective-permute-done((bf16[256,512]{1,0:T(8,128)(2,1)}, bf16[256,512]{1,0:T(8,128)(2,1)S(1)}, u32[]{:S(2)}, u32[]{:S(2)}) %collective-permute-start.29) | collective-permute-done | bytes 262176 | tf_op jit(solution)/shard_map/ppermute | solution.py:44
  112.4 1.3 collective-permute-start.30
  115.2 2.9 %collective-permute-done.25.refs_9_ = bf16[256,512]{1,0:T(8,128)(2,1)S(1)} collective-permute-done((bf16[256,512]{1,0:T(8,128)(2,1)}, bf16[256,512]{1,0:T(8,128)(2,1)S(1)}, u32[]{:S(2)}, u32[]{:S(2)}) %collective-permute-start.25) | collective-permute-done | bytes 262176 | tf_op jit(solution)/shard_map/ppermute | solution.py:44
  118.1 1.7 collective-permute-done.22.refs_8_
  120.5 10.4 %attend.2 = (bf16[512,256]{1,0:T(8,128)(2,1)}, bf16[512,256]{1,0:T(8,128)(2,1)}, bf16[512,256]{1,0:T(8,128)(2,1)}, bf16[512,256]{1,0:T(8,128)(2,1)}, bf16[256,51...) custom-call(s32[33]{0:T(128)} %pad_add_fusion.3.slot_ref, ...), custom_call_target="tpu_custom_call" | custom-call | flops 2684354560 | bytes 4194304 | tf_op jit(solution)/shard_map/attend/pallas_call | solution.py:393
  130.9 1.4 collective-permute-start.39
  136.5 3.4 %collective-permute-done.31.refs_9_ = bf16[256,512]{1,0:T(8,128)(2,1)S(1)} collective-permute-done((bf16[256,512]{1,0:T(8,128)(2,1)S(1)}, bf16[256,512]{1,0:T(8,128)(2,1)S(1)}, u32[]{:S(2)}, u32[]{:S(2)}) %collective-permute-start.31) | collective-permute-done | bytes 262176 | tf_op jit(solution)/shard_map/ppermute | solution.py:44
  139.9 1.3 collective-permute-start.32
  141.3 1.3 collective-permute-start.40
  143.0 5.0 %collective-permute-done.32.refs_8_ = bf16[256,512]{1,0:T(8,128)(2,1)S(1)} collective-permute-done((bf16[256,512]{1,0:T(8,128)(2,1)S(1)}, bf16[256,512]{1,0:T(8,128)(2,1)S(1)}, u32[]{:S(2)}, u32[]{:S(2)}) %collective-permute-start.32) | collective-permute-done | bytes 262176 | tf_op jit(solution)/shard_map/ppermute | solution.py:44
  148.7 10.4 %attend.3 = (bf16[512,256]{1,0:T(8,128)(2,1)}, bf16[512,256]{1,0:T(8,128)(2,1)}, bf16[512,256]{1,0:T(8,128)(2,1)}, bf16[512,256]{1,0:T(8,128)(2,1)}, bf16[256,51...) custom-call(s32[33]{0:T(128)} %pad_add_fusion.3.slot_ref, ...), custom_call_target="tpu_custom_call" | custom-call | flops 2684354560 | bytes 4194304 | tf_op jit(solution)/shard_map/attend/pallas_call | solution.py:393
  159.1 1.4 collective-permute-start.45
  160.7 1.5 collective-permute-start.41
  162.6 7.6 %collective-permute-start.34 = (bf16[512,512]{1,0:T(8,128)(2,1)S(1)}, bf16[512,512]{1,0:T(8,128)(2,1)S(1)}, u32[]{:S(2)}, u32[]{:S(2)}) collective-permute-start(bf16[512,512]{1,0:T(8,128)(2,1)S(1)} %pad_maximum_fusion.5), channel_id=1, source_target_pairs={{0,2},{2,0},{1,3},{3,1},{4,6},{6,4},{5,7},{7,5},{8,10},{10,8},{9,1... | collective-permute-start | bytes 1572872 | tf_op jit(solution)/shard_map/ppermute | solution.py:47
  170.4 1.8 collective-permute-start.33
  172.3 1.4 collective-permute-start.46
  174.3 4.4 %collective-permute-done.46 = bf16[256,512]{1,0:T(8,128)(2,1)S(1)} collective-permute-done((bf16[256,512]{1,0:T(8,128)(2,1)S(1)}, bf16[256,512]{1,0:T(8,128)(2,1)S(1)}, u32[]{:S(2)}, u32[]{:S(2)}) %collective-permute-start.46) | collective-permute-done | bytes 262176 | tf_op jit(solution)/shard_map/ppermute | solution.py:44
  178.8 1.6 collective-permute-start.47
  180.6 3.8 %collective-permute-done.47 = bf16[256,512]{1,0:T(8,128)(2,1)S(1)} collective-permute-done((bf16[256,512]{1,0:T(8,128)(2,1)S(1)}, bf16[256,512]{1,0:T(8,128)(2,1)S(1)}, u32[]{:S(2)}, u32[]{:S(2)}) %collective-permute-start.47) | collective-permute-done | bytes 262176 | tf_op jit(solution)/shard_map/ppermute | solution.py:44
  184.4 2.6 %collective-permute-start.48 = (bf16[256,512]{1,0:T(8,128)(2,1)S(1)}, bf16[256,512]{1,0:T(8,128)(2,1)S(1)}, u32[]{:S(2)}, u32[]{:S(2)}) collective-permute-start(bf16[256,512]{1,0:T(8,128)(2,1)S(1)} %add_convert_fusion.1), channel_id=1, source_target_pairs={{8,0},{16,8},{24,16},{28,24},{20,28},{12,20},{4,12},{0,4},{9,1},{1... | collective-permute-start | bytes 786440 | tf_op jit(solution)/shard_map/ppermute | solution.py:44
  191.0 7.4 %state.2 = (f32[2048,128]{1,0:T(8,128)}, bf16[2048,128]{1,0:T(8,128)(2,1)}) custom-call(s32[18]{0:T(128)} %pad_add_fusion.4.info_ref, bf16[256,512]{1,0:T(8,128)(2,1)} %after.5.refs_0_, bf16[256,512]{1,0:T(8,128)(2,1)} %copy-done.19, bf16[256,512]{1,0:T(8,128)(2,1)} %copy-done.18, bf16[256,512]{1,0:T(8,128)(2,1)} %get-tuple-element.51.refs_3_, ...), custom_call_target="tpu_custom_call" | custom-call | flops 1 | bytes 1 | tf_op jit(solution)/shard_map/state/pallas_call | solution.py:205
  198.5 3.8 %collective-permute-start.49 = (bf16[2048,128]{1,0:T(8,128)(2,1)}, bf16[2048,128]{1,0:T(8,128)(2,1)S(1)}, u32[]{:S(2)}, u32[]{:S(2)}) collective-permute-start(bf16[2048,128]{1,0:T(8,128)(2,1)} %get-tuple-element.60), channel_id=1, source_target_pairs={{0,2},{2,0},{1,3},{3,1},{4,6},{6,4},{5,7},{7,5},{8,10},{10,8},{9,1... | collective-permute-start | bytes 1572872 | tf_op jit(solution)/shard_map/ppermute | solution.py:47
  202.3 1.7 collective-permute-done.49
  204.0 1.3 add_convert_fusion.refs_1_
  206.3 7.1 %state.3 = (f32[2048,128]{1,0:T(8,128)}, bf16[2048,128]{1,0:T(8,128)(2,1)}) custom-call(s32[18]{0:T(128)} %pad_add_fusion.4.info_ref, bf16[256,512]{1,0:T(8,128)(2,1)} %after.6.refs_0_, bf16[256,512]{1,0:T(8,128)(2,1)} %copy-done.19, bf16[256,512]{1,0:T(8,128)(2,1)} %copy-done.18, bf16[256,512]{1,0:T(8,128)(2,1)} %get-tuple-element.51.refs_3_, ...), custom_call_target="tpu_custom_call" | custom-call | flops 1 | bytes 1 | tf_op jit(solution)/shard_map/state/pallas_call | solution.py:205
  214.2 4.4 %collective-permute-done.51.refs_0_ = bf16[2048,128]{1,0:T(8,128)(2,1)S(1)} collective-permute-done((bf16[2048,128]{1,0:T(8,128)(2,1)S(1)}, bf16[2048,128]{1,0:T(8,128)(2,1)S(1)}, u32[]{:S(2)}, u32[]{:S(2)}) %collective-permute-start.51) | collective-permute-done | bytes 524320 | tf_op jit(solution)/shard_map/ppermute | solution.py:514
  (233 shorter events, 38.3 us)
Async XLA Ops:
  2.9 13.6 %collective-permute-start.4 = (bf16[256,1024]{1,0:T(8,128)(2,1)S(1)}, bf16[256,1024]{1,0:T(8,128)(2,1)S(1)}, u32[]{:S(2)}, u32[]{:S(2)}) collective-permute-start(bf16[256,1024]{1,0:T(8,128)(2,1)S(1)} %pad_maximum_fusion.2.refs_0_.refs_6_), channel_id=1, source_target_pairs={{0,8},{8,16},{16,24},{24,28},{28,20},{20,12},{12,4},{4,0},{1,9},{9... | collective-permute-start | bytes 1572872 | tf_op jit(solution)/shard_map/ppermute | solution.py:41
  4.4 13.1 %collective-permute-start.12 = (bf16[256,1024]{1,0:T(8,128)(2,1)S(1)}, bf16[256,1024]{1,0:T(8,128)(2,1)S(1)}, u32[]{:S(2)}, u32[]{:S(2)}) collective-permute-start(bf16[256,1024]{1,0:T(8,128)(2,1)S(1)} %collective-permute-done.7.refs_1_.refs_7_), channel_id=1, source_target_pairs={{8,0},{16,8},{24,16},{28,24},{20,28},{12,20},{4,12},{0,4},{9,1},{1... | collective-permute-start | bytes 1572872 | tf_op jit(solution)/shard_map/ppermute | solution.py:44
  5.7 23.2 %collective-permute-start.16 = (bf16[256,1024]{1,0:T(8,128)(2,1)S(1)}, bf16[256,1024]{1,0:T(8,128)(2,1)S(1)}, u32[]{:S(2)}, u32[]{:S(2)}) collective-permute-start(bf16[256,1024]{1,0:T(8,128)(2,1)S(1)} %pad_maximum_fusion.2.refs_0_.refs_6_), channel_id=1, source_target_pairs={{8,0},{16,8},{24,16},{28,24},{20,28},{12,20},{4,12},{0,4},{9,1},{1... | collective-permute-start | bytes 1572872 | tf_op jit(solution)/shard_map/ppermute | solution.py:44
  7.0 56.9 %collective-permute-start.3 = (bf16[128,4096]{1,0:T(8,128)(2,1)}, bf16[128,4096]{1,0:T(8,128)(2,1)}, u32[]{:S(2)}, u32[]{:S(2)}) collective-permute-start(bf16[128,4096]{1,0:T(8,128)(2,1)} %bitcast.7), channel_id=1, source_target_pairs={{0,2},{2,0},{1,3},{3,1},{4,6},{6,4},{5,7},{7,5},{8,10},{10,8},{9,1... | collective-permute-start | bytes 3145736 | tf_op jit(solution)/shard_map/ppermute | solution.py:47
  8.6 21.6 %collective-permute-start.8 = (bf16[256,1024]{1,0:T(8,128)(2,1)S(1)}, bf16[256,1024]{1,0:T(8,128)(2,1)S(1)}, u32[]{:S(2)}, u32[]{:S(2)}) collective-permute-start(bf16[256,1024]{1,0:T(8,128)(2,1)S(1)} %collective-permute-done.7.refs_1_.refs_7_), channel_id=1, source_target_pairs={{0,8},{8,16},{16,24},{24,28},{28,20},{20,12},{12,4},{4,0},{1,9},{9... | collective-permute-start | bytes 1572872 | tf_op jit(solution)/shard_map/ppermute | solution.py:41
  16.5 22.6 %collective-permute-start.5 = (bf16[256,1024]{1,0:T(8,128)(2,1)S(1)}, bf16[256,1024]{1,0:T(8,128)(2,1)}, u32[]{:S(2)}, u32[]{:S(2)}) collective-permute-start(bf16[256,1024]{1,0:T(8,128)(2,1)S(1)} %collective-permute-done.4.refs_2_.refs_8_), channel_id=1, source_target_pairs={{0,8},{8,16},{16,24},{24,28},{28,20},{20,12},{12,4},{4,0},{1,9},{9... | collective-permute-start | bytes 1572872 | tf_op jit(solution)/shard_map/ppermute | solution.py:41
  17.5 22.6 %collective-permute-start.13 = (bf16[256,1024]{1,0:T(8,128)(2,1)S(1)}, bf16[256,1024]{1,0:T(8,128)(2,1)}, u32[]{:S(2)}, u32[]{:S(2)}) collective-permute-start(bf16[256,1024]{1,0:T(8,128)(2,1)S(1)} %collective-permute-done.12.refs_9_.refs_21_), channel_id=1, source_target_pairs={{8,0},{16,8},{24,16},{28,24},{20,28},{12,20},{4,12},{0,4},{9,1},{1... | collective-permute-start | bytes 1572872 | tf_op jit(solution)/shard_map/ppermute | solution.py:44
  28.9 22.5 %collective-permute-start.17 = (bf16[256,1024]{1,0:T(8,128)(2,1)S(1)}, bf16[256,1024]{1,0:T(8,128)(2,1)}, u32[]{:S(2)}, u32[]{:S(2)}) collective-permute-start(bf16[256,1024]{1,0:T(8,128)(2,1)S(1)} %collective-permute-done.16.refs_8_.refs_20_), channel_id=1, source_target_pairs={{8,0},{16,8},{24,16},{28,24},{20,28},{12,20},{4,12},{0,4},{9,1},{1... | collective-permute-start | bytes 1572872 | tf_op jit(solution)/shard_map/ppermute | solution.py:44
  30.2 22.5 %collective-permute-start.9 = (bf16[256,1024]{1,0:T(8,128)(2,1)S(1)}, bf16[256,1024]{1,0:T(8,128)(2,1)}, u32[]{:S(2)}, u32[]{:S(2)}) collective-permute-start(bf16[256,1024]{1,0:T(8,128)(2,1)S(1)} %collective-permute-done.8.refs_3_.refs_9_), channel_id=1, source_target_pairs={{0,8},{8,16},{16,24},{24,28},{28,20},{20,12},{12,4},{4,0},{1,9},{9... | collective-permute-start | bytes 1572872 | tf_op jit(solution)/shard_map/ppermute | solution.py:41
  39.1 22.5 %collective-permute-start.6 = (bf16[256,1024]{1,0:T(8,128)(2,1)}, bf16[256,1024]{1,0:T(8,128)(2,1)}, u32[]{:S(2)}, u32[]{:S(2)}) collective-permute-start(bf16[256,1024]{1,0:T(8,128)(2,1)} %collective-permute-done.5.refs_4_.refs_10_), channel_id=1, source_target_pairs={{0,8},{8,16},{16,24},{24,28},{28,20},{20,12},{12,4},{4,0},{1,9},{9... | collective-permute-start | bytes 1572872 | tf_op jit(solution)/shard_map/ppermute | solution.py:41
  40.1 22.5 %collective-permute-start.14 = (bf16[256,1024]{1,0:T(8,128)(2,1)}, bf16[256,1024]{1,0:T(8,128)(2,1)}, u32[]{:S(2)}, u32[]{:S(2)}) collective-permute-start(bf16[256,1024]{1,0:T(8,128)(2,1)} %collective-permute-done.13.refs_7_.refs_19_), channel_id=1, source_target_pairs={{8,0},{16,8},{24,16},{28,24},{20,28},{12,20},{4,12},{0,4},{9,1},{1... | collective-permute-start | bytes 1572872 | tf_op jit(solution)/shard_map/ppermute | solution.py:44
  51.3 22.4 %collective-permute-start.18 = (bf16[256,1024]{1,0:T(8,128)(2,1)}, bf16[256,1024]{1,0:T(8,128)(2,1)S(1)}, u32[]{:S(2)}, u32[]{:S(2)}) collective-permute-start(bf16[256,1024]{1,0:T(8,128)(2,1)} %collective-permute-done.17.refs_6_.refs_18_), channel_id=1, source_target_pairs={{8,0},{16,8},{24,16},{28,24},{20,28},{12,20},{4,12},{0,4},{9,1},{1... | collective-permute-start | bytes 1572872 | tf_op jit(solution)/shard_map/ppermute | solution.py:44
  52.6 21.1 %collective-permute-start.10 = (bf16[256,1024]{1,0:T(8,128)(2,1)}, bf16[256,1024]{1,0:T(8,128)(2,1)S(1)}, u32[]{:S(2)}, u32[]{:S(2)}) collective-permute-start(bf16[256,1024]{1,0:T(8,128)(2,1)} %collective-permute-done.9.refs_5_.refs_11_), channel_id=1, source_target_pairs={{0,8},{8,16},{16,24},{24,28},{28,20},{20,12},{12,4},{4,0},{1,9},{9... | collective-permute-start | bytes 1572872 | tf_op jit(solution)/shard_map/ppermute | solution.py:41
  61.6 22.4 %collective-permute-start.11 = (bf16[256,1024]{1,0:T(8,128)(2,1)}, bf16[256,1024]{1,0:T(8,128)(2,1)S(1)}, u32[]{:S(2)}, u32[]{:S(2)}) collective-permute-start(bf16[256,1024]{1,0:T(8,128)(2,1)} %collective-permute-done.6.refs_0_.refs_12_), channel_id=1, source_target_pairs={{0,8},{8,16},{16,24},{24,28},{28,20},{20,12},{12,4},{4,0},{1,9},{9... | collective-permute-start | bytes 1572872 | tf_op jit(solution)/shard_map/ppermute | solution.py:41
  62.6 22.4 %collective-permute-start.15 = (bf16[256,1024]{1,0:T(8,128)(2,1)}, bf16[256,1024]{1,0:T(8,128)(2,1)S(1)}, u32[]{:S(2)}, u32[]{:S(2)}) collective-permute-start(bf16[256,1024]{1,0:T(8,128)(2,1)} %collective-permute-done.14.refs_5_.refs_17_), channel_id=1, source_target_pairs={{8,0},{16,8},{24,16},{28,24},{20,28},{12,20},{4,12},{0,4},{9,1},{1... | collective-permute-start | bytes 1572872 | tf_op jit(solution)/shard_map/ppermute | solution.py:44
  87.8 6.7 %collective-permute-start.19 = (bf16[256,512]{1,0:T(8,128)(2,1)S(1)}, bf16[256,512]{1,0:T(8,128)(2,1)S(1)}, u32[]{:S(2)}, u32[]{:S(2)}) collective-permute-start(bf16[256,512]{1,0:T(8,128)(2,1)S(1)} %get-tuple-element.33.refs_4_), channel_id=1, source_target_pairs={{0,8},{8,16},{16,24},{24,28},{28,20},{20,12},{12,4},{4,0},{1,9},{9... | collective-permute-start | bytes 786440 | tf_op jit(solution)/shard_map/ppermute | solution.py:41
  88.1 9.4 %collective-permute-start.23 = (bf16[256,512]{1,0:T(8,128)(2,1)S(1)}, bf16[256,512]{1,0:T(8,128)(2,1)S(1)}, u32[]{:S(2)}, u32[]{:S(2)}) collective-permute-start(bf16[256,512]{1,0:T(8,128)(2,1)S(1)} %get-tuple-element.33.refs_4_), channel_id=1, source_target_pairs={{8,0},{16,8},{24,16},{28,24},{20,28},{12,20},{4,12},{0,4},{9,1},{1... | collective-permute-start | bytes 786440 | tf_op jit(solution)/shard_map/ppermute | solution.py:44
  89.4 9.5 %collective-permute-start = (s32[8,3]{0,1:T(4,128)S(1)}, s32[8,3]{0,1:T(4,128)S(1)}, u32[]{:S(2)}, u32[]{:S(2)}) collective-permute-start(s32[8,3]{0,1:T(4,128)S(1)} %get-tuple-element.77), channel_id=1, source_target_pairs={{0,2},{2,0},{1,3},{3,1},{4,6},{6,4},{5,7},{7,5},{8,10},{10,8},{9,1... | collective-permute-start | bytes 296 | tf_op jit(solution)/shard_map/ppermute | solution.py:47
  94.7 13.3 %collective-permute-start.1 = (bf16[512,512]{1,0:T(8,128)(2,1)S(1)}, bf16[512,512]{1,0:T(8,128)(2,1)S(1)}, u32[]{:S(2)}, u32[]{:S(2)}) collective-permute-start(bf16[512,512]{1,0:T(8,128)(2,1)S(1)} %constant_dynamic-slice_fusion.9), channel_id=1, source_target_pairs={{0,2},{2,0},{1,3},{3,1},{4,6},{6,4},{5,7},{7,5},{8,10},{10,8},{9,1... | collective-permute-start | bytes 1572872 | tf_op jit(solution)/shard_map/ppermute | solution.py:47
  97.2 17.9 %collective-permute-start.2 = (bf16[512,512]{1,0:T(8,128)(2,1)S(1)}, bf16[512,512]{1,0:T(8,128)(2,1)S(1)}, u32[]{:S(2)}, u32[]{:S(2)}) collective-permute-start(bf16[512,512]{1,0:T(8,128)(2,1)S(1)} %constant_dynamic-slice_fusion.8), channel_id=1, source_target_pairs={{0,2},{2,0},{1,3},{3,1},{4,6},{6,4},{5,7},{7,5},{8,10},{10,8},{9,1... | collective-permute-start | bytes 1572872 | tf_op jit(solution)/shard_map/ppermute | solution.py:47
  97.5 7.5 %collective-permute-start.24 = (bf16[256,512]{1,0:T(8,128)(2,1)S(1)}, bf16[256,512]{1,0:T(8,128)(2,1)S(1)}, u32[]{:S(2)}, u32[]{:S(2)}) collective-permute-start(bf16[256,512]{1,0:T(8,128)(2,1)S(1)} %collective-permute-done.23.refs_11_), channel_id=1, source_target_pairs={{8,0},{16,8},{24,16},{28,24},{20,28},{12,20},{4,12},{0,4},{9,1},{1... | collective-permute-start | bytes 786440 | tf_op jit(solution)/shard_map/ppermute | solution.py:44
  100.2 9.1 %collective-permute-start.21 = (bf16[256,512]{1,0:T(8,128)(2,1)S(1)}, bf16[256,512]{1,0:T(8,128)(2,1)}, u32[]{:S(2)}, u32[]{:S(2)}) collective-permute-start(bf16[256,512]{1,0:T(8,128)(2,1)S(1)} %collective-permute-done.20.refs_6_.refs_1_), channel_id=1, source_target_pairs={{0,8},{8,16},{16,24},{24,28},{28,20},{20,12},{12,4},{4,0},{1,9},{9... | collective-permute-start | bytes 786440 | tf_op jit(solution)/shard_map/ppermute | solution.py:41
  105.7 6.7 %collective-permute-start.29 = (bf16[256,512]{1,0:T(8,128)(2,1)}, bf16[256,512]{1,0:T(8,128)(2,1)S(1)}, u32[]{:S(2)}, u32[]{:S(2)}) collective-permute-start(bf16[256,512]{1,0:T(8,128)(2,1)} %after.4.refs_4_), channel_id=1, source_target_pairs={{8,0},{16,8},{24,16},{28,24},{20,28},{12,20},{4,12},{0,4},{9,1},{1... | collective-permute-start | bytes 786440 | tf_op jit(solution)/shard_map/ppermute | solution.py:44
  107.8 7.2 %collective-permute-start.26 = (bf16[256,512]{1,0:T(8,128)(2,1)}, bf16[256,512]{1,0:T(8,128)(2,1)}, u32[]{:S(2)}, u32[]{:S(2)}) collective-permute-start(bf16[256,512]{1,0:T(8,128)(2,1)} %after.4.refs_4_), channel_id=1, source_target_pairs={{0,8},{8,16},{16,24},{24,28},{28,20},{20,12},{12,4},{4,0},{1,9},{9... | collective-permute-start | bytes 786440 | tf_op jit(solution)/shard_map/ppermute | solution.py:41
  108.0 10.1 %collective-permute-start.25 = (bf16[256,512]{1,0:T(8,128)(2,1)}, bf16[256,512]{1,0:T(8,128)(2,1)S(1)}, u32[]{:S(2)}, u32[]{:S(2)}) collective-permute-start(bf16[256,512]{1,0:T(8,128)(2,1)} %copy-done.39), channel_id=1, source_target_pairs={{8,0},{16,8},{24,16},{28,24},{20,28},{12,20},{4,12},{0,4},{9,1},{1... | collective-permute-start | bytes 786440 | tf_op jit(solution)/shard_map/ppermute | solution.py:44
  109.3 10.5 %collective-permute-start.22 = (bf16[256,512]{1,0:T(8,128)(2,1)}, bf16[256,512]{1,0:T(8,128)(2,1)S(1)}, u32[]{:S(2)}, u32[]{:S(2)}) collective-permute-start(bf16[256,512]{1,0:T(8,128)(2,1)} %collective-permute-done.21.refs_7_), channel_id=1, source_target_pairs={{0,8},{8,16},{16,24},{24,28},{28,20},{20,12},{12,4},{4,0},{1,9},{9... | collective-permute-start | bytes 786440 | tf_op jit(solution)/shard_map/ppermute | solution.py:41
  112.4 19.9 %collective-permute-start.30 = (bf16[256,512]{1,0:T(8,128)(2,1)S(1)}, bf16[256,512]{1,0:T(8,128)(2,1)S(1)}, u32[]{:S(2)}, u32[]{:S(2)}) collective-permute-start(bf16[256,512]{1,0:T(8,128)(2,1)S(1)} %collective-permute-done.29.refs_11_), channel_id=1, source_target_pairs={{8,0},{16,8},{24,16},{28,24},{20,28},{12,20},{4,12},{0,4},{9,1},{1... | collective-permute-start | bytes 786440 | tf_op jit(solution)/shard_map/ppermute | solution.py:44
  115.0 21.3 %collective-permute-start.27 = (bf16[256,512]{1,0:T(8,128)(2,1)}, bf16[256,512]{1,0:T(8,128)(2,1)}, u32[]{:S(2)}, u32[]{:S(2)}) collective-permute-start(bf16[256,512]{1,0:T(8,128)(2,1)} %collective-permute-done.26.refs_5_), channel_id=1, source_target_pairs={{0,8},{8,16},{16,24},{24,28},{28,20},{20,12},{12,4},{4,0},{1,9},{9... | collective-permute-start | bytes 786440 | tf_op jit(solution)/shard_map/ppermute | solution.py:41
  130.9 10.3 %collective-permute-start.39 = (bf16[256,512]{1,0:T(8,128)(2,1)}, bf16[256,512]{1,0:T(8,128)(2,1)S(1)}, u32[]{:S(2)}, u32[]{:S(2)}) collective-permute-start(bf16[256,512]{1,0:T(8,128)(2,1)} %get-tuple-element.50), channel_id=1, source_target_pairs={{8,0},{16,8},{24,16},{28,24},{20,28},{12,20},{4,12},{0,4},{9,1},{1... | collective-permute-start | bytes 786440 | tf_op jit(solution)/shard_map/ppermute | solution.py:44
  132.3 7.6 %collective-permute-start.31 = (bf16[256,512]{1,0:T(8,128)(2,1)S(1)}, bf16[256,512]{1,0:T(8,128)(2,1)S(1)}, u32[]{:S(2)}, u32[]{:S(2)}) collective-permute-start(bf16[256,512]{1,0:T(8,128)(2,1)S(1)} %collective-permute-done.30.refs_10_), channel_id=1, source_target_pairs={{8,0},{16,8},{24,16},{28,24},{20,28},{12,20},{4,12},{0,4},{9,1},{1... | collective-permute-start | bytes 786440 | tf_op jit(solution)/shard_map/ppermute | solution.py:44
  134.2 8.4 %collective-permute-start.35 = (bf16[256,512]{1,0:T(8,128)(2,1)}, bf16[256,512]{1,0:T(8,128)(2,1)S(1)}, u32[]{:S(2)}, u32[]{:S(2)}) collective-permute-start(bf16[256,512]{1,0:T(8,128)(2,1)} %get-tuple-element.47), channel_id=1, source_target_pairs={{0,8},{8,16},{16,24},{24,28},{28,20},{20,12},{12,4},{4,0},{1,9},{9... | collective-permute-start | bytes 786440 | tf_op jit(solution)/shard_map/ppermute | solution.py:41
  136.3 6.6 %collective-permute-start.28 = (bf16[256,512]{1,0:T(8,128)(2,1)}, bf16[256,512]{1,0:T(8,128)(2,1)S(1)}, u32[]{:S(2)}, u32[]{:S(2)}) collective-permute-start(bf16[256,512]{1,0:T(8,128)(2,1)} %collective-permute-done.27.refs_6_), channel_id=1, source_target_pairs={{0,8},{8,16},{16,24},{24,28},{28,20},{20,12},{12,4},{4,0},{1,9},{9... | collective-permute-start | bytes 786440 | tf_op jit(solution)/shard_map/ppermute | solution.py:41
  139.9 8.1 %collective-permute-start.32 = (bf16[256,512]{1,0:T(8,128)(2,1)S(1)}, bf16[256,512]{1,0:T(8,128)(2,1)S(1)}, u32[]{:S(2)}, u32[]{:S(2)}) collective-permute-start(bf16[256,512]{1,0:T(8,128)(2,1)S(1)} %collective-permute-done.31.refs_9_), channel_id=1, source_target_pairs={{8,0},{16,8},{24,16},{28,24},{20,28},{12,20},{4,12},{0,4},{9,1},{1... | collective-permute-start | bytes 786440 | tf_op jit(solution)/shard_map/ppermute | solution.py:44
  141.3 19.4 %collective-permute-start.40 = (bf16[256,512]{1,0:T(8,128)(2,1)S(1)}, bf16[256,512]{1,0:T(8,128)(2,1)S(1)}, u32[]{:S(2)}, u32[]{:S(2)}) collective-permute-start(bf16[256,512]{1,0:T(8,128)(2,1)S(1)} %add_convert_fusion.7), channel_id=1, source_target_pairs={{8,0},{16,8},{24,16},{28,24},{20,28},{12,20},{4,12},{0,4},{9,1},{1... | collective-permute-start | bytes 786440 | tf_op jit(solution)/shard_map/ppermute | solution.py:44
  142.7 19.5 %collective-permute-start.36 = (bf16[256,512]{1,0:T(8,128)(2,1)S(1)}, bf16[256,512]{1,0:T(8,128)(2,1)S(1)}, u32[]{:S(2)}, u32[]{:S(2)}) collective-permute-start(bf16[256,512]{1,0:T(8,128)(2,1)S(1)} %add_convert_fusion.10), channel_id=1, source_target_pairs={{0,8},{8,16},{16,24},{24,28},{28,20},{20,12},{12,4},{4,0},{1,9},{9... | collective-permute-start | bytes 786440 | tf_op jit(solution)/shard_map/ppermute | solution.py:41
  159.1 11.3 %collective-permute-start.45 = (bf16[256,512]{1,0:T(8,128)(2,1)}, bf16[256,512]{1,0:T(8,128)(2,1)S(1)}, u32[]{:S(2)}, u32[]{:S(2)}) collective-permute-start(bf16[256,512]{1,0:T(8,128)(2,1)} %get-tuple-element.58), channel_id=1, source_target_pairs={{8,0},{16,8},{24,16},{28,24},{20,28},{12,20},{4,12},{0,4},{9,1},{1... | collective-permute-start | bytes 786440 | tf_op jit(solution)/shard_map/ppermute | solution.py:44
  160.5 11.8 %collective-permute-start.42 = (bf16[256,512]{1,0:T(8,128)(2,1)}, bf16[256,512]{1,0:T(8,128)(2,1)S(1)}, u32[]{:S(2)}, u32[]{:S(2)}) collective-permute-start(bf16[256,512]{1,0:T(8,128)(2,1)} %get-tuple-element.54), channel_id=1, source_target_pairs={{0,8},{8,16},{16,24},{24,28},{28,20},{20,12},{12,4},{4,0},{1,9},{9... | collective-permute-start | bytes 786440 | tf_op jit(solution)/shard_map/ppermute | solution.py:41
  160.7 28.5 %collective-permute-start.41 = (bf16[256,512]{1,0:T(8,128)(2,1)S(1)}, bf16[256,512]{1,0:T(8,128)(2,1)S(1)}, u32[]{:S(2)}, u32[]{:S(2)}) collective-permute-start(bf16[256,512]{1,0:T(8,128)(2,1)S(1)} %add_convert_fusion.6), channel_id=1, source_target_pairs={{8,0},{16,8},{24,16},{28,24},{20,28},{12,20},{4,12},{0,4},{9,1},{1... | collective-permute-start | bytes 786440 | tf_op jit(solution)/shard_map/ppermute | solution.py:44
  162.3 11.4 %collective-permute-start.37 = (bf16[256,512]{1,0:T(8,128)(2,1)S(1)}, bf16[256,512]{1,0:T(8,128)(2,1)S(1)}, u32[]{:S(2)}, u32[]{:S(2)}) collective-permute-start(bf16[256,512]{1,0:T(8,128)(2,1)S(1)} %add_convert_fusion.9), channel_id=1, source_target_pairs={{0,8},{8,16},{16,24},{24,28},{28,20},{20,12},{12,4},{4,0},{1,9},{9... | collective-permute-start | bytes 786440 | tf_op jit(solution)/shard_map/ppermute | solution.py:41
  162.6 11.4 %collective-permute-start.34 = (bf16[512,512]{1,0:T(8,128)(2,1)S(1)}, bf16[512,512]{1,0:T(8,128)(2,1)S(1)}, u32[]{:S(2)}, u32[]{:S(2)}) collective-permute-start(bf16[512,512]{1,0:T(8,128)(2,1)S(1)} %pad_maximum_fusion.5), channel_id=1, source_target_pairs={{0,2},{2,0},{1,3},{3,1},{4,6},{6,4},{5,7},{7,5},{8,10},{10,8},{9,1... | collective-permute-start | bytes 1572872 | tf_op jit(solution)/shard_map/ppermute | solution.py:47
  170.4 9.9 %collective-permute-start.33 = (bf16[512,512]{1,0:T(8,128)(2,1)S(1)}, bf16[512,512]{1,0:T(8,128)(2,1)S(1)}, u32[]{:S(2)}, u32[]{:S(2)}) collective-permute-start(bf16[512,512]{1,0:T(8,128)(2,1)S(1)} %pad_maximum_fusion.4), channel_id=1, source_target_pairs={{0,2},{2,0},{1,3},{3,1},{4,6},{6,4},{5,7},{7,5},{8,10},{10,8},{9,1... | collective-permute-start | bytes 1572872 | tf_op jit(solution)/shard_map/ppermute | solution.py:47
  172.3 6.4 %collective-permute-start.46 = (bf16[256,512]{1,0:T(8,128)(2,1)S(1)}, bf16[256,512]{1,0:T(8,128)(2,1)S(1)}, u32[]{:S(2)}, u32[]{:S(2)}) collective-permute-start(bf16[256,512]{1,0:T(8,128)(2,1)S(1)} %add_convert_fusion.3), channel_id=1, source_target_pairs={{8,0},{16,8},{24,16},{28,24},{20,28},{12,20},{4,12},{0,4},{9,1},{1... | collective-permute-start | bytes 786440 | tf_op jit(solution)/shard_map/ppermute | solution.py:44
  173.7 6.7 %collective-permute-start.43 = (bf16[256,512]{1,0:T(8,128)(2,1)S(1)}, bf16[256,512]{1,0:T(8,128)(2,1)S(1)}, u32[]{:S(2)}, u32[]{:S(2)}) collective-permute-start(bf16[256,512]{1,0:T(8,128)(2,1)S(1)} %add_convert_fusion.5), channel_id=1, source_target_pairs={{0,8},{8,16},{16,24},{24,28},{28,20},{20,12},{12,4},{4,0},{1,9},{9... | collective-permute-start | bytes 786440 | tf_op jit(solution)/shard_map/ppermute | solution.py:41
  174.0 15.2 %collective-permute-start.38 = (bf16[256,512]{1,0:T(8,128)(2,1)S(1)}, bf16[256,512]{1,0:T(8,128)(2,1)S(1)}, u32[]{:S(2)}, u32[]{:S(2)}) collective-permute-start(bf16[256,512]{1,0:T(8,128)(2,1)S(1)} %add_convert_fusion.8), channel_id=1, source_target_pairs={{0,8},{8,16},{16,24},{24,28},{28,20},{20,12},{12,4},{4,0},{1,9},{9... | collective-permute-start | bytes 786440 | tf_op jit(solution)/shard_map/ppermute | solution.py:41
  180.5 9.5 %collective-permute-start.44 = (bf16[256,512]{1,0:T(8,128)(2,1)S(1)}, bf16[256,512]{1,0:T(8,128)(2,1)S(1)}, u32[]{:S(2)}, u32[]{:S(2)}) collective-permute-start(bf16[256,512]{1,0:T(8,128)(2,1)S(1)} %add_convert_fusion.4), channel_id=1, source_target_pairs={{0,8},{8,16},{16,24},{24,28},{28,20},{20,12},{12,4},{4,0},{1,9},{9... | collective-permute-start | bytes 786440 | tf_op jit(solution)/shard_map/ppermute | solution.py:41
  184.4 5.9 %collective-permute-start.48 = (bf16[256,512]{1,0:T(8,128)(2,1)S(1)}, bf16[256,512]{1,0:T(8,128)(2,1)S(1)}, u32[]{:S(2)}, u32[]{:S(2)}) collective-permute-start(bf16[256,512]{1,0:T(8,128)(2,1)S(1)} %add_convert_fusion.1), channel_id=1, source_target_pairs={{8,0},{16,8},{24,16},{28,24},{20,28},{12,20},{4,12},{0,4},{9,1},{1... | collective-permute-start | bytes 786440 | tf_op jit(solution)/shard_map/ppermute | solution.py:44
  205.4 13.2 %collective-permute-start.51 = (bf16[2048,128]{1,0:T(8,128)(2,1)S(1)}, bf16[2048,128]{1,0:T(8,128)(2,1)S(1)}, u32[]{:S(2)}, u32[]{:S(2)}) collective-permute-start(bf16[2048,128]{1,0:T(8,128)(2,1)S(1)} %add_convert_fusion.refs_1_), channel_id=1, source_target_pairs={{0,1},{1,0},{2,3},{3,2},{4,5},{5,4},{6,7},{7,6},{8,9},{9,8},{10,11... | collective-permute-start | bytes 1572872 | tf_op jit(solution)/shard_map/ppermute | solution.py:514
  213.4 5.9 %collective-permute-start.50 = (bf16[2048,128]{1,0:T(8,128)(2,1)}, bf16[2048,128]{1,0:T(8,128)(2,1)S(1)}, u32[]{:S(2)}, u32[]{:S(2)}) collective-permute-start(bf16[2048,128]{1,0:T(8,128)(2,1)} %get-tuple-element.62), channel_id=1, source_target_pairs={{0,2},{2,0},{1,3},{3,1},{4,6},{6,4},{5,7},{7,5},{8,10},{10,8},{9,1... | collective-permute-start | bytes 1572872 | tf_op jit(solution)/shard_map/ppermute | solution.py:47
  (59 other events, 688.6 us)
